TPU v7x, 512 devices: a whole 4x8x8 slice. The times are simulated.
512 devices in a mesh: pts: 16 (over y, core), dir: 16 (over x, z_hi), freq: 2 (over z_lo).
Axes of the slice: x: 4, y: 8, z: 8 (z_hi: 4, z_lo: 2; z = z_hi * 2 + z_lo), core: 2. Of those that a mesh axis runs over, the one named last changes fastest.
Arguments:
- action: float32 [48, 64, 65536], P('freq', 'dir', 'pts'), may hold values from 0.05 to 2
- bathymetry: float32 [65536], P('pts'), may hold values from 20 to 60
- refraction: float32 [48, 65536], P('freq', 'pts'), may hold values from 0.5 to 2
- shifting: float32 [48, 65536], P('freq', 'pts'), may hold values from 0.5 to 2
- heading: float32 [65536], P('pts'), may hold values from -3.140625 to 3.140625
- slope_angle: float32 [65536], P('pts'), may hold values from -3.140625 to 3.140625
- wet_mask: int32 [65536], P('pts'), may hold values 0 or 1
- substeps: int32 [128], P('pts'), may hold values from 1 to 4
Outputs:
- evolved: float32 [48, 64, 65536], P('freq', 'dir', 'pts')
All inputs are finite; a program needn't handle non-finite values. Where the computation divides by a largest or mean magnitude, that divisor is 1e-20 or more. No bound on the sum of `wet_mask` on one device may be relied on, other than what follows from the above.
Results may differ from a plain program's by a relative error of at most 0.00002.
Values sent between devices are 32-bit elements; how exact they have to be, the bound alone decides.
No kernel may reach another device: no remote copies, remote signals or barrier semaphores. Data moves between devices by JAX's collectives and lax.ppermute only.
A program may use at most 64 MiB of HBM per device.

v0:
```python
import math

import jax
import jax.numpy as jnp
from jax import lax
from jax.sharding import Mesh
from jax.sharding import PartitionSpec as P

FREQ = 48
DIR = 64
KMAX = 4
BLK = 512
PTS = ("pts_0", "pts_1")
PTS_FREQ = ("pts_0", "pts_1", "freq")


EPSILON = 1e-06


def with_halo(cells, sides, width, closed):
    for axis, dim in sides:
        count = lax.axis_size(axis)
        ends = count if closed else count - 1
        head = lax.slice_in_dim(cells, 0, width, axis=dim)
        tail = lax.slice_in_dim(cells, cells.shape[dim] - width, cells.shape[dim], axis=dim)
        cells = jnp.concatenate(
            [
                lax.ppermute(tail, axis, [(i, (i + 1) % count) for i in range(ends)]),
                cells,
                lax.ppermute(head, axis, [((i + 1) % count, i) for i in range(ends)]),
            ],
            axis=dim,
        )
    return cells


def by_axis(value, axes):
    for axis in axes:
        value = lax.pmax(value, axis)
    return value


def sweep(values, courant, weight, active, along):
    extent = values.shape[along]
    lower_cells = lax.slice_in_dim(values, 0, extent - 1, axis=along)
    upper_cells = lax.slice_in_dim(values, 1, extent, axis=along)
    interface = (
        0.5
        * (
            lax.slice_in_dim(courant, 0, extent - 1, axis=along)
            + lax.slice_in_dim(courant, 1, extent, axis=along)
        )
        * weight
    )
    fluxes = jnp.maximum(interface, 0.0) * lower_cells + jnp.minimum(interface, 0.0) * upper_cells
    change = lax.slice_in_dim(fluxes, 1, extent - 1, axis=along) - lax.slice_in_dim(
        fluxes, 0, extent - 2, axis=along
    )
    inner_cells = lax.slice_in_dim(values, 1, extent - 1, axis=along)
    return jnp.where(active, inner_cells - change, inner_cells)


def direction_angles(index):
    return (index.astype(jnp.float32) + 0.5) * (2.0 * math.pi / DIR)


def local(action, bathymetry, refraction, shifting, heading, slope_angle, wet_mask, substeps):
    freq_local, dir_local, points = action.shape
    rimmed = with_halo(bathymetry, ((PTS, 0),), 1, False)
    position = lax.axis_index(PTS)
    last_block = lax.axis_size(PTS) - 1
    left_depth = jnp.where(position == 0, bathymetry[:1], rimmed[:1])
    right_depth = jnp.where(position == last_block, bathymetry[-1:], rimmed[-1:])
    padded = jnp.concatenate([left_depth, bathymetry, right_depth])
    gradient = (padded[2:] - padded[:-2]) * 0.5
    wet_float = wet_mask.astype(jnp.float32)
    turn_base = refraction * gradient[None, :] * wet_float[None, :]
    shift_base = shifting * wet_float[None, :]
    dir_start = lax.axis_index("dir") * dir_local
    local_angles = direction_angles(dir_start + jnp.arange(dir_local, dtype=jnp.int32))
    cosines = jnp.cos(local_angles[:, None] - heading[None, :])
    c_shift = shift_base[:, None, :] * cosines[None, :, :]
    all_angles = direction_angles(jnp.arange(DIR, dtype=jnp.int32))
    cos_peak = jnp.max(jnp.abs(jnp.cos(all_angles[:, None] - heading[None, :])), axis=0)
    sin_peak = jnp.max(jnp.abs(jnp.sin(all_angles[:, None] - slope_angle[None, :])), axis=0)
    local_turn = jnp.max(jnp.abs(turn_base) * sin_peak[None, :])
    local_shift = jnp.max(jnp.abs(shift_base) * cos_peak[None, :])
    peak_turn, peak_shift = (by_axis(local_turn, PTS_FREQ), by_axis(local_shift, PTS_FREQ))
    scale_turn = 0.5 / (peak_turn + EPSILON)
    scale_shift = 0.5 / (peak_shift + EPSILON)
    point_counts = jnp.broadcast_to(substeps[:, None], (substeps.shape[0], BLK)).reshape(-1)
    count_float = point_counts.astype(jnp.float32)
    spectrum = action
    wrap_index = jnp.mod(dir_start - KMAX + jnp.arange(dir_local + 2 * KMAX, dtype=jnp.int32), DIR)
    sine_wrap = jnp.sin(direction_angles(wrap_index)[:, None] - slope_angle[None, :])
    courant_deep = (
        turn_base[:, None, :] * sine_wrap[None, :, :] * scale_turn / count_float[None, None, :]
    )
    wrapped = with_halo(spectrum, (("dir", 1),), KMAX, True)
    for sweep_index in range(KMAX):
        active = (sweep_index < point_counts)[None, None, :]
        width_now = dir_local + 2 * (KMAX - sweep_index)
        courant_now = courant_deep[:, sweep_index : sweep_index + width_now]
        wrapped = sweep(wrapped, courant_now, 1.0, active, 1)
    spectrum = wrapped
    courant_shift = c_shift * scale_shift / count_float[None, None, :]
    courant_chain = with_halo(courant_shift, (("freq", 0),), 1, False)
    chain_index = (
        lax.axis_index("freq") * freq_local - 1 + jnp.arange(freq_local + 2, dtype=jnp.int32)
    )
    valid_faces = (chain_index[:-1] >= 0) & (chain_index[1:] <= FREQ - 1)
    freq_weight = jnp.where(valid_faces, 1.0, 0.0).astype(jnp.float32)[:, None, None]
    for sweep_index in range(KMAX):
        active = (sweep_index < point_counts)[None, None, :]
        chained = with_halo(spectrum, (("freq", 0),), 1, False)
        spectrum = sweep(chained, courant_chain, freq_weight, active, 0)
    return spectrum * wet_float[None, None, :]


def solution(mesh):
    torus = Mesh(
        mesh.devices.reshape(8, 2, mesh.shape["dir"], mesh.shape["freq"]),
        ("pts_0", "pts_1", "dir", "freq"),
    )
    in_specs = (
        P("freq", "dir", PTS),
        P(PTS),
        P("freq", PTS),
        P("freq", PTS),
        P(PTS),
        P(PTS),
        P(PTS),
        P(PTS),
    )
    out_specs = P("freq", "dir", PTS)
    return jax.shard_map(local, mesh=torus, in_specs=in_specs, out_specs=out_specs, check_vma=False)
```

profile of v0, /device:TPU:56, one launch (start us, length us, event | category | flops | bytes accessed | tf_op | source)
XLA Modules:
  0.0 155.7 jit_solution(4419694682905386786)
XLA Ops:
  0.0 6.2 %collective-permute-start = (f32[24,4,4096]{2,1,0:T(4,128)}, f32[24,4,4096]{2,1,0:T(4,128)S(1)}, u32[]{:S(2)}, u32[]{:S(2)}) collective-permute-start(f32[24,4,4096]{2,1,0:T(4,128)} %param.8), channel_id=1, source_target_pairs={{0,2},{2,4},{4,6},{6,8},{8,10},{10,12},{12,14},{14,16},{16,18},{18... | collective-permute-start | bytes 4718600 | tf_op jit(solution)/shard_map/ppermute | solution.py:28
  6.2 9.0 %collective-permute-start.1 = (f32[24,4,4096]{2,1,0:T(4,128)}, f32[24,4,4096]{2,1,0:T(4,128)}, u32[]{:S(2)}, u32[]{:S(2)}) collective-permute-start(f32[24,4,4096]{2,1,0:T(4,128)} %param.8), channel_id=1, source_target_pairs={{2,0},{4,2},{6,4},{8,6},{10,8},{12,10},{14,12},{16,14},{18,16},{20... | collective-permute-start | bytes 4718600 | tf_op jit(solution)/shard_map/ppermute | solution.py:30
  15.2 1.4 fusion.26
  16.6 2.4 %collective-permute-start.2 = (f32[1]{0:T(128)}, f32[1]{0:T(128)}, u32[]{:S(2)}, u32[]{:S(2)}) collective-permute-start(f32[1]{0:T(128)} %get-tuple-element.30), channel_id=1, source_target_pairs={{32,0},{64,32},{96,64},{128,96},{160,128},{192,160},{224,192},{256... | collective-permute-start | bytes 20 | tf_op jit(solution)/shard_map/ppermute | solution.py:30
  19.0 2.5 %collective-permute-start.3 = (f32[1]{0:T(128)}, f32[1]{0:T(128)}, u32[]{:S(2)}, u32[]{:S(2)}) collective-permute-start(f32[1]{0:T(128)} %get-tuple-element.29), channel_id=1, source_target_pairs={{0,32},{32,64},{64,96},{96,128},{128,160},{160,192},{192,224},{224... | collective-permute-start | bytes 20 | tf_op jit(solution)/shard_map/ppermute | solution.py:28
  21.5 0.7 convert_element_type.40
  22.1 0.7 broadcast_compare_fusion.3
  22.8 0.7 convert_element_type.37
  23.5 0.1 broadcast_bitcast_fusion
  23.6 0.1 broadcast_bitcast_fusion.1
  23.7 0.1 broadcast_bitcast_fusion.3
  23.8 1.6 %subtract_sine_fusion = f32[12,4096]{1,0:T(8,128)S(1)} fusion(f32[4096]{0:T(1024)} %param.13, f32[12]{0:T(128)S(1)} %fusion.18), kind=kLoop, calls=%fused_computation.59 | loop fusion | flops 49152 | bytes 213040 | tf_op jit(solution)/shard_map/sin | solution.py:95
  25.5 8.0 %abs_reduce_fusion = (f32[4096]{0:T(1024)S(1)}, f32[4096]{0:T(1024)S(1)}) fusion(f32[4096]{0:T(1024)} %param.12, f32[64]{0:T(128)S(1)} %add_multiply_fusion.1, f32[4096]{0:T(1024)} %param.13), kind=kLoop, calls=%fused_computation.54 | loop fusion | flops 1564672 | bytes 65792 | tf_op jit(solution)/shard_map/reduce_max | solution.py:84
  33.5 1.2 subtract_cosine_fusion
  34.7 0.6 iota_add_fusion
  35.3 0.0 collective-permute-done.2
  36.7 0.0 collective-permute-done.3
  37.9 0.9 fusion.15
  38.8 0.8 multiply_reduce_fusion
  39.5 15.1 %all-reduce = (f32[]{:T(128)}, f32[]{:T(128)}) all-reduce(f32[]{:T(128)} %get-tuple-element.27, f32[]{:T(128)} %get-tuple-element.13), channel_id=1, replica_groups=mesh['pts_0'=8,'pts_1'=2,'dir'=16,'freq'=2] {'pts_0'}, use_global_device_ids=true, to_apply=%region_2.3 | all-reduce | flops 2 | bytes 16 | tf_op jit(solution)/shard_map/pmax | solution.py:39
  54.6 3.1 %all-reduce.2 = (f32[]{:T(128)}, f32[]{:T(128)}) all-reduce(f32[]{:T(128)} %get-tuple-element.7, f32[]{:T(128)} %get-tuple-element.8), channel_id=1, replica_groups=mesh['pts_0'=8,'pts_1'=2,'dir'=16,'freq'=2] {'pts_1'}, use_global_device_ids=true, to_apply=%region_3.4 | all-reduce | flops 2 | bytes 16 | tf_op jit(solution)/shard_map/pmax | solution.py:39
  57.7 26.8 %all-reduce.1 = (f32[]{:T(128)}, f32[]{:T(128)}) all-reduce(f32[]{:T(128)} %get-tuple-element.11, f32[]{:T(128)} %get-tuple-element.12), channel_id=1, replica_groups=mesh['pts_0'=8,'pts_1'=2,'dir'=16,'freq'=2] {'freq'}, use_global_device_ids=true, to_apply=%region_4.5 | all-reduce | flops 2 | bytes 16 | tf_op jit(solution)/shard_map/pmax | solution.py:39
  85.9 0.5 multiply_divide_fusion.1
  86.4 0.0 copy-start
  86.4 1.5 collective-permute-start.4
  87.9 1.5 collective-permute-start.5
  89.4 0.0 copy-start.2
  89.4 1.0 multiply_divide_fusion
  90.4 0.4 copy-done.2
  90.8 2.5 %pad_maximum_fusion = f32[24,12,4096]{2,1,0:T(8,128)S(1)} fusion(f32[24,4,4096]{2,1,0:T(4,128)} %collective-permute-done.1, f32[24,4,4096]{2,1,0:T(4,128)S(1)} %copy-done.2, f32[24,4,4096]{2,1,0:T(4,128)S(1)} %collective-permute-done), kind=kLoop, calls=%fused_computation.12 | loop fusion | flops 2359296 | bytes 9437184 | tf_op jit(solution)/shard_map/concatenate | solution.py:26
  93.4 2.3 %fusion.2 = f32[24,11,4096]{2,1,0:T(8,128)S(1)} fusion(f32[24,12,4096]{2,1,0:T(8,128)S(1)} %pad_maximum_fusion, f32[24,12,4096]{2,1,0:T(8,128)S(1)} %multiply_divide_fusion), kind=kLoop, calls=%fused_computation.8 | loop fusion | flops 7569408 | bytes 21626880 | tf_op jit(solution)/shard_map/add | solution.py:55
  95.7 2.0 %subtract_select_fusion = f32[24,10,4096]{2,1,0:T(8,128)S(1)} fusion(f32[24,11,4096]{2,1,0:T(8,128)S(1)} %fusion.2, f32[24,12,4096]{2,1,0:T(8,128)S(1)} %pad_maximum_fusion, pred[4096]{0:T(1024)(128)(4,1)S(1)} %bitcast.25), kind=kLoop, calls=%fused_computation | loop fusion | flops 2949120 | bytes 15732736 | tf_op jit(solution)/shard_map/jit(_where)/select_n | solution.py:60
  97.7 4.4 %fusion = f32[24,9,4096]{2,1,0:T(8,128)} fusion(f32[24,10,4096]{2,1,0:T(8,128)S(1)} %subtract_select_fusion, f32[24,12,4096]{2,1,0:T(8,128)S(1)} %multiply_divide_fusion), kind=kLoop, calls=%fused_computation.2 | loop fusion | flops 6193152 | bytes 17694720 | tf_op jit(solution)/shard_map/add | solution.py:55
  102.1 5.3 %subtract_select_fusion.2 = f32[24,8,4096]{2,1,0:T(8,128)S(1)} fusion(f32[24,9,4096]{2,1,0:T(8,128)} %fusion, f32[24,10,4096]{2,1,0:T(8,128)S(1)} %subtract_select_fusion, pred[4096]{0:T(1024)(128)(4,1)S(1)} %bitcast.21), kind=kLoop, calls=%fused_computation.15 | loop fusion | flops 2359296 | bytes 12587008 | tf_op jit(solution)/shard_map/jit(_where)/select_n | solution.py:60
  107.4 1.4 fusion.6
  108.8 0.7 subtract_select_fusion.1
  109.5 1.3 fusion.4
  110.9 0.0 copy-start.1
  110.9 0.8 subtract_select_fusion.7
  111.7 4.5 %collective-permute-start.6 = (f32[1,4,4096]{2,1,0:T(4,128)S(1)}, f32[1,4,4096]{2,1,0:T(4,128)S(1)}, u32[]{:S(2)}, u32[]{:S(2)}) collective-permute-start(f32[1,4,4096]{2,1,0:T(4,128)S(1)} %get-tuple-element.26), channel_id=1, source_target_pairs={{0,1},{2,3},{4,5},{6,7},{8,9},{10,11},{12,13},{14,15},{16,17},{18,... | collective-permute-start | bytes 196616 | tf_op jit(solution)/shard_map/ppermute | solution.py:28
  116.3 1.5 collective-permute-start.7
  117.8 0.1 fusion.20
  117.9 0.3 collective-permute-done.6
  118.1 4.3 %collective-permute-done.7 = f32[1,4,4096]{2,1,0:T(4,128)S(1)} collective-permute-done((f32[1,4,4096]{2,1,0:T(4,128)S(1)}, f32[1,4,4096]{2,1,0:T(4,128)S(1)}, u32[]{:S(2)}, u32[]{:S(2)}) %collective-permute-start.7) | collective-permute-done | bytes 65568 | tf_op jit(solution)/shard_map/ppermute | solution.py:30
  122.4 1.7 %fusion.9 = f32[25,4,4096]{2,1,0:T(4,128)S(1)} fusion(f32[24,4,4096]{2,1,0:T(4,128)S(1)} %subtract_select_fusion.7, f32[1,4,4096]{2,1,0:T(4,128)S(1)} %collective-permute-done.6, f32[1,4,4096]{2,1,0:T(4,128)S(1)} %collective-permute-done.7, f32[25]{0:T(128)S(1)} %fusion.20, f32[1,4,4096]{2,1,0:T(4,128)S(1)} %collective-permute-done.5, ...), kind=kLoop, calls=%fused_computation.36 | loop fusion | flops 4505600 | bytes 5046372 | tf_op jit(solution)/shard_map/add | solution.py:55
  124.1 0.5 subtract_select_fusion.6
  124.6 1.6 %collective-permute-start.8 = (f32[1,4,4096]{2,1,0:T(4,128)S(1)}, f32[1,4,4096]{2,1,0:T(4,128)S(1)}, u32[]{:S(2)}, u32[]{:S(2)}) collective-permute-start(f32[1,4,4096]{2,1,0:T(4,128)S(1)} %get-tuple-element.22), channel_id=1, source_target_pairs={{0,1},{2,3},{4,5},{6,7},{8,9},{10,11},{12,13},{14,15},{16,17},{18,... | collective-permute-start | bytes 196616 | tf_op jit(solution)/shard_map/ppermute | solution.py:28
  126.2 1.3 collective-permute-start.9
  127.5 0.6 collective-permute-done.8
  128.1 4.3 %collective-permute-done.9 = f32[1,4,4096]{2,1,0:T(4,128)S(1)} collective-permute-done((f32[1,4,4096]{2,1,0:T(4,128)S(1)}, f32[1,4,4096]{2,1,0:T(4,128)S(1)}, u32[]{:S(2)}, u32[]{:S(2)}) %collective-permute-start.9) | collective-permute-done | bytes 65568 | tf_op jit(solution)/shard_map/ppermute | solution.py:30
  132.3 1.7 %fusion.10 = f32[25,4,4096]{2,1,0:T(4,128)S(1)} fusion(f32[24,4,4096]{2,1,0:T(4,128)S(1)} %subtract_select_fusion.6, f32[1,4,4096]{2,1,0:T(4,128)S(1)} %collective-permute-done.8, f32[1,4,4096]{2,1,0:T(4,128)S(1)} %collective-permute-done.9, f32[25]{0:T(128)S(1)} %fusion.20, f32[1,4,4096]{2,1,0:T(4,128)S(1)} %collective-permute-done.5, ...), kind=kLoop, calls=%fused_computation.39 | loop fusion | flops 4505600 | bytes 5046372 | tf_op jit(solution)/shard_map/add | solution.py:55
  134.0 0.5 subtract_select_fusion.5
  134.5 1.6 %collective-permute-start.10 = (f32[1,4,4096]{2,1,0:T(4,128)S(1)}, f32[1,4,4096]{2,1,0:T(4,128)S(1)}, u32[]{:S(2)}, u32[]{:S(2)}) collective-permute-start(f32[1,4,4096]{2,1,0:T(4,128)S(1)} %get-tuple-element.20), channel_id=1, source_target_pairs={{0,1},{2,3},{4,5},{6,7},{8,9},{10,11},{12,13},{14,15},{16,17},{18,... | collective-permute-start | bytes 196616 | tf_op jit(solution)/shard_map/ppermute | solution.py:28
  136.1 1.3 collective-permute-start.11
  137.4 0.6 collective-permute-done.10
  138.0 4.3 %collective-permute-done.11 = f32[1,4,4096]{2,1,0:T(4,128)S(1)} collective-permute-done((f32[1,4,4096]{2,1,0:T(4,128)S(1)}, f32[1,4,4096]{2,1,0:T(4,128)S(1)}, u32[]{:S(2)}, u32[]{:S(2)}) %collective-permute-start.11) | collective-permute-done | bytes 65568 | tf_op jit(solution)/shard_map/ppermute | solution.py:30
  142.3 1.7 %fusion.11 = f32[25,4,4096]{2,1,0:T(4,128)S(1)} fusion(f32[24,4,4096]{2,1,0:T(4,128)S(1)} %subtract_select_fusion.5, f32[1,4,4096]{2,1,0:T(4,128)S(1)} %collective-permute-done.10, f32[1,4,4096]{2,1,0:T(4,128)S(1)} %collective-permute-done.11, f32[25]{0:T(128)S(1)} %fusion.20, f32[1,4,4096]{2,1,0:T(4,128)S(1)} %collective-permute-done.5, ...), kind=kLoop, calls=%fused_computation.42 | loop fusion | flops 4505600 | bytes 5046372 | tf_op jit(solution)/shard_map/add | solution.py:55
  143.9 0.7 subtract_select_fusion.4
  144.6 1.6 %collective-permute-start.12 = (f32[1,4,4096]{2,1,0:T(4,128)S(1)}, f32[1,4,4096]{2,1,0:T(4,128)S(1)}, u32[]{:S(2)}, u32[]{:S(2)}) collective-permute-start(f32[1,4,4096]{2,1,0:T(4,128)S(1)} %get-tuple-element.18), channel_id=1, source_target_pairs={{0,1},{2,3},{4,5},{6,7},{8,9},{10,11},{12,13},{14,15},{16,17},{18,... | collective-permute-start | bytes 196616 | tf_op jit(solution)/shard_map/ppermute | solution.py:28
  146.2 1.3 collective-permute-start.13
  147.5 0.6 collective-permute-done.12
  148.1 4.3 %collective-permute-done.13 = f32[1,4,4096]{2,1,0:T(4,128)S(1)} collective-permute-done((f32[1,4,4096]{2,1,0:T(4,128)S(1)}, f32[1,4,4096]{2,1,0:T(4,128)S(1)}, u32[]{:S(2)}, u32[]{:S(2)}) %collective-permute-start.13) | collective-permute-done | bytes 65568 | tf_op jit(solution)/shard_map/ppermute | solution.py:30
  152.3 1.7 %fusion.12 = f32[25,4,4096]{2,1,0:T(4,128)S(1)} fusion(f32[24,4,4096]{2,1,0:T(4,128)S(1)} %subtract_select_fusion.4, f32[1,4,4096]{2,1,0:T(4,128)S(1)} %collective-permute-done.12, f32[1,4,4096]{2,1,0:T(4,128)S(1)} %collective-permute-done.13, f32[25]{0:T(128)S(1)} %fusion.20, f32[1,4,4096]{2,1,0:T(4,128)S(1)} %collective-permute-done.5, ...), kind=kLoop, calls=%fused_computation.45 | loop fusion | flops 4505600 | bytes 5046372 | tf_op jit(solution)/shard_map/add | solution.py:55
  154.0 1.7 %fusion.13 = f32[24,4,4096]{2,1,0:T(4,128)} fusion(f32[24,4,4096]{2,1,0:T(4,128)S(1)} %subtract_select_fusion.4, f32[25,4,4096]{2,1,0:T(4,128)S(1)} %fusion.12, f32[4096]{0:T(1024)S(1)} %convert_element_type.37, pred[4096]{0:T(1024)(128)(4,1)S(1)} %bitcast.24), kind=kLoop, calls=%fused_computation.47 | loop fusion | flops 1572864 | bytes 6311936 | tf_op jit(solution)/shard_map/mul | solution.py:117
  (25 shorter events, 0.1 us)
Async XLA Ops:
  0.0 38.7 %copy-start.4 = (f32[24,4096]{1,0:T(8,128)S(1)}, f32[24,4096]{1,0:T(8,128)}, u32[]{:S(2)}) copy-start(f32[24,4096]{1,0:T(8,128)} %param.10) | copy-start | bytes 1179652
  0.0 38.7 %copy-start.3 = (f32[24,4096]{1,0:T(8,128)S(1)}, f32[24,4096]{1,0:T(8,128)}, u32[]{:S(2)}) copy-start(f32[24,4096]{1,0:T(8,128)} %param.11) | copy-start | bytes 1179652
  0.0 90.4 %collective-permute-start = (f32[24,4,4096]{2,1,0:T(4,128)}, f32[24,4,4096]{2,1,0:T(4,128)S(1)}, u32[]{:S(2)}, u32[]{:S(2)}) collective-permute-start(f32[24,4,4096]{2,1,0:T(4,128)} %param.8), channel_id=1, source_target_pairs={{0,2},{2,4},{4,6},{6,8},{8,10},{10,12},{12,14},{14,16},{16,18},{18... | collective-permute-start | bytes 4718600 | tf_op jit(solution)/shard_map/ppermute | solution.py:28
  6.2 84.2 %collective-permute-start.1 = (f32[24,4,4096]{2,1,0:T(4,128)}, f32[24,4,4096]{2,1,0:T(4,128)}, u32[]{:S(2)}, u32[]{:S(2)}) collective-permute-start(f32[24,4,4096]{2,1,0:T(4,128)} %param.8), channel_id=1, source_target_pairs={{2,0},{4,2},{6,4},{8,6},{10,8},{12,10},{14,12},{16,14},{18,16},{20... | collective-permute-start | bytes 4718600 | tf_op jit(solution)/shard_map/ppermute | solution.py:30
  16.6 18.8 %collective-permute-start.2 = (f32[1]{0:T(128)}, f32[1]{0:T(128)}, u32[]{:S(2)}, u32[]{:S(2)}) collective-permute-start(f32[1]{0:T(128)} %get-tuple-element.30), channel_id=1, source_target_pairs={{32,0},{64,32},{96,64},{128,96},{160,128},{192,160},{224,192},{256... | collective-permute-start | bytes 20 | tf_op jit(solution)/shard_map/ppermute | solution.py:30
  19.0 17.7 %collective-permute-start.3 = (f32[1]{0:T(128)}, f32[1]{0:T(128)}, u32[]{:S(2)}, u32[]{:S(2)}) collective-permute-start(f32[1]{0:T(128)} %get-tuple-element.29), channel_id=1, source_target_pairs={{0,32},{32,64},{64,96},{96,128},{128,160},{160,192},{192,224},{224... | collective-permute-start | bytes 20 | tf_op jit(solution)/shard_map/ppermute | solution.py:28
  86.4 3.0 %copy-start = (f32[24,4,4096]{2,1,0:T(4,128)}, f32[24,4,4096]{2,1,0:T(4,128)S(1)}, u32[]{:S(2)}) copy-start(f32[24,4,4096]{2,1,0:T(4,128)S(1)} %multiply_divide_fusion.1) | copy-start | bytes 4718596
  86.4 31.4 %collective-permute-start.4 = (f32[1,4,4096]{2,1,0:T(4,128)S(1)}, f32[1,4,4096]{2,1,0:T(4,128)S(1)}, u32[]{:S(2)}, u32[]{:S(2)}) collective-permute-start(f32[1,4,4096]{2,1,0:T(4,128)S(1)} %get-tuple-element.23), channel_id=1, source_target_pairs={{0,1},{2,3},{4,5},{6,7},{8,9},{10,11},{12,13},{14,15},{16,17},{18,... | collective-permute-start | bytes 196616 | tf_op jit(solution)/shard_map/ppermute | solution.py:28
  87.9 29.9 %collective-permute-start.5 = (f32[1,4,4096]{2,1,0:T(4,128)S(1)}, f32[1,4,4096]{2,1,0:T(4,128)S(1)}, u32[]{:S(2)}, u32[]{:S(2)}) collective-permute-start(f32[1,4,4096]{2,1,0:T(4,128)S(1)} %get-tuple-element.24), channel_id=1, source_target_pairs={{1,0},{3,2},{5,4},{7,6},{9,8},{11,10},{13,12},{15,14},{17,16},{19,... | collective-permute-start | bytes 196616 | tf_op jit(solution)/shard_map/ppermute | solution.py:30
  89.4 1.4 copy-start.2
  110.8 6.9 %copy-start.5 = (s32[26]{0:T(128)S(1)}, s32[26]{0:T(128)}, u32[]{:S(2)}) copy-start(s32[26]{0:T(128)} %iota_add_fusion) | copy-start | bytes 316
  110.9 11.6 %copy-start.1 = (f32[24,4,4096]{2,1,0:T(4,128)S(1)}, f32[24,4,4096]{2,1,0:T(4,128)}, u32[]{:S(2)}) copy-start(f32[24,4,4096]{2,1,0:T(4,128)} %copy-done) | copy-start | bytes 4718596
  111.7 6.4 %collective-permute-start.6 = (f32[1,4,4096]{2,1,0:T(4,128)S(1)}, f32[1,4,4096]{2,1,0:T(4,128)S(1)}, u32[]{:S(2)}, u32[]{:S(2)}) collective-permute-start(f32[1,4,4096]{2,1,0:T(4,128)S(1)} %get-tuple-element.26), channel_id=1, source_target_pairs={{0,1},{2,3},{4,5},{6,7},{8,9},{10,11},{12,13},{14,15},{16,17},{18,... | collective-permute-start | bytes 196616 | tf_op jit(solution)/shard_map/ppermute | solution.py:28
  116.3 6.2 %collective-permute-start.7 = (f32[1,4,4096]{2,1,0:T(4,128)S(1)}, f32[1,4,4096]{2,1,0:T(4,128)S(1)}, u32[]{:S(2)}, u32[]{:S(2)}) collective-permute-start(f32[1,4,4096]{2,1,0:T(4,128)S(1)} %get-tuple-element.25), channel_id=1, source_target_pairs={{1,0},{3,2},{5,4},{7,6},{9,8},{11,10},{13,12},{15,14},{17,16},{19,... | collective-permute-start | bytes 196616 | tf_op jit(solution)/shard_map/ppermute | solution.py:30
  124.6 3.5 %collective-permute-start.8 = (f32[1,4,4096]{2,1,0:T(4,128)S(1)}, f32[1,4,4096]{2,1,0:T(4,128)S(1)}, u32[]{:S(2)}, u32[]{:S(2)}) collective-permute-start(f32[1,4,4096]{2,1,0:T(4,128)S(1)} %get-tuple-element.22), channel_id=1, source_target_pairs={{0,1},{2,3},{4,5},{6,7},{8,9},{10,11},{12,13},{14,15},{16,17},{18,... | collective-permute-start | bytes 196616 | tf_op jit(solution)/shard_map/ppermute | solution.py:28
  126.2 6.2 %collective-permute-start.9 = (f32[1,4,4096]{2,1,0:T(4,128)S(1)}, f32[1,4,4096]{2,1,0:T(4,128)S(1)}, u32[]{:S(2)}, u32[]{:S(2)}) collective-permute-start(f32[1,4,4096]{2,1,0:T(4,128)S(1)} %get-tuple-element.21), channel_id=1, source_target_pairs={{1,0},{3,2},{5,4},{7,6},{9,8},{11,10},{13,12},{15,14},{17,16},{19,... | collective-permute-start | bytes 196616 | tf_op jit(solution)/shard_map/ppermute | solution.py:30
  134.5 3.5 %collective-permute-start.10 = (f32[1,4,4096]{2,1,0:T(4,128)S(1)}, f32[1,4,4096]{2,1,0:T(4,128)S(1)}, u32[]{:S(2)}, u32[]{:S(2)}) collective-permute-start(f32[1,4,4096]{2,1,0:T(4,128)S(1)} %get-tuple-element.20), channel_id=1, source_target_pairs={{0,1},{2,3},{4,5},{6,7},{8,9},{10,11},{12,13},{14,15},{16,17},{18,... | collective-permute-start | bytes 196616 | tf_op jit(solution)/shard_map/ppermute | solution.py:28
  136.1 6.2 %collective-permute-start.11 = (f32[1,4,4096]{2,1,0:T(4,128)S(1)}, f32[1,4,4096]{2,1,0:T(4,128)S(1)}, u32[]{:S(2)}, u32[]{:S(2)}) collective-permute-start(f32[1,4,4096]{2,1,0:T(4,128)S(1)} %get-tuple-element.19), channel_id=1, source_target_pairs={{1,0},{3,2},{5,4},{7,6},{9,8},{11,10},{13,12},{15,14},{17,16},{19,... | collective-permute-start | bytes 196616 | tf_op jit(solution)/shard_map/ppermute | solution.py:30
  144.6 3.5 %collective-permute-start.12 = (f32[1,4,4096]{2,1,0:T(4,128)S(1)}, f32[1,4,4096]{2,1,0:T(4,128)S(1)}, u32[]{:S(2)}, u32[]{:S(2)}) collective-permute-start(f32[1,4,4096]{2,1,0:T(4,128)S(1)} %get-tuple-element.18), channel_id=1, source_target_pairs={{0,1},{2,3},{4,5},{6,7},{8,9},{10,11},{12,13},{14,15},{16,17},{18,... | collective-permute-start | bytes 196616 | tf_op jit(solution)/shard_map/ppermute | solution.py:28
  146.2 6.2 %collective-permute-start.13 = (f32[1,4,4096]{2,1,0:T(4,128)S(1)}, f32[1,4,4096]{2,1,0:T(4,128)S(1)}, u32[]{:S(2)}, u32[]{:S(2)}) collective-permute-start(f32[1,4,4096]{2,1,0:T(4,128)S(1)} %get-tuple-element.17), channel_id=1, source_target_pairs={{1,0},{3,2},{5,4},{7,6},{9,8},{11,10},{13,12},{15,14},{17,16},{19,... | collective-permute-start | bytes 196616 | tf_op jit(solution)/shard_map/ppermute | solution.py:30
where the time goes:
time: 157 us; the launch traced here: 156 us
  other arithmetic  47.4 us (30%)
  blocking collectives  45 us (29%)
  starting transfers between devices  37.7 us (24%)
  waiting for transfers between devices  19.1 us (12%)
  between operations  4.38 us (3%)
  local copies, waits for them, and re-layouts  2.13 us (1%)
    pmax x3, blocking collectives, by_axis(): value = lax.pmax(value, axis)  45 us
    ppermute x7, starting transfers between devices, with_halo(): lax.ppermute(tail, axis, [(i, (i + 1) % count) for i in range(ends)])  19.5 us
    ppermute x7, starting transfers between devices, with_halo(): lax.ppermute(head, axis, [((i + 1) % count, i) for i in range(ends)])  18.2 us
    ppermute x7, waiting for transfers between devices, with_halo(): lax.ppermute(head, axis, [((i + 1) % count, i) for i in range(ends)])  17.1 us
    add x8, other arithmetic, sweep(): jnp.maximum(interface, 0.0) * lower_cells  16 us
    select_n x7, other arithmetic, sweep(): return jnp.where(active, inner_cells - change, inner_cells)  10.5 us
    reduce_max x1, other arithmetic, local(): jnp.max(jnp.abs(jnp.cos(all_angles[:, None] - heading[None, :])), axis=0)  8.03 us
  transfers between devices with their start and end apart: 14, of which 8 were waited for; matrix products, arithmetic and copies ran while one was open for 25% of the time, Pallas kernels for 0%

commit v1 on v0

v1 whole, which is shorter than its diff:
```python
import functools
import math

import jax
import jax.numpy as jnp
import numpy as np
from jax import lax
from jax.experimental import pallas as pl
from jax.experimental.pallas import tpu as pltpu
from jax.sharding import Mesh
from jax.sharding import PartitionSpec as P

FREQ = 48
DIR = 64
KMAX = 4
BLK = 512
SLOTS = 256
EPSILON = 1e-06
LANES = 128
F_LOC = 24
D_LOC = 4
TILES = 32
ROWS = TILES * D_LOC
VMEM_LIMIT = 24 * 1024 * 1024

f32, bf16, i32 = jnp.float32, jnp.bfloat16, jnp.int32


def angle_table():
    step = 2.0 * math.pi / DIR
    half = np.arange(DIR // 2) * step
    centre = (np.arange(DIR // 2) + 0.5) * step
    parts = [np.sin(half), np.cos(half), np.sin(centre), np.cos(centre)]
    return np.concatenate([np.concatenate([p, -p]) for p in parts]).astype(np.float32)


SIN_FACE, COS_FACE, SIN_CELL, COS_CELL = 0, DIR, 2 * DIR, 3 * DIR
COS_HALF = math.cos(math.pi / DIR)


def iota(shape, dim):
    return lax.broadcasted_iota(i32, shape, dim)


def shifted(bath):
    lane = iota((TILES, LANES), 1)
    left = pltpu.roll(bath, 1, 1)
    left = jnp.where(lane == 0, pltpu.roll(left, 1, 0), left)
    right = pltpu.roll(bath, LANES - 1, 1)
    right = jnp.where(lane == LANES - 1, pltpu.roll(right, TILES - 1, 0), right)
    return left, right


def end_points():
    point = iota((TILES, LANES), 0) * LANES + iota((TILES, LANES), 1)
    return point == 0, point == TILES * LANES - 1


def full_gradient(meta, bath, below, above):
    left, right = shifted(bath)
    first, last = end_points()
    from_below, _ = shifted(below)
    _, from_above = shifted(above)
    lo = jnp.where(meta[2] == 0, bath, from_below)
    hi = jnp.where(meta[2] == 15, bath, from_above)
    return (jnp.where(last, hi, right) - jnp.where(first, lo, left)) * 0.5


def face_sine(table, face, sin_s, cos_s):
    at = lax.rem(face + DIR, DIR)
    return table[SIN_FACE + at] * cos_s - table[COS_FACE + at] * sin_s


def masks(table, meta, bath, slope, wet):
    left, right = shifted(bath)
    drive = (right - left) * wet
    first, last = end_points()
    ends = first | last
    sin_s, cos_s = jnp.sin(slope), jnp.cos(slope)

    def at(face):
        speed = drive * face_sine(table, face, sin_s, cos_s)
        return (speed > 0.0) | ends, (speed < 0.0) | ends

    return at


def ranks(mask):
    on = jnp.where(mask, 1.0, 0.0).astype(f32)
    row, col = iota((LANES, LANES), 0), iota((LANES, LANES), 1)
    before = jnp.where(row < col, 1.0, 0.0).astype(bf16)
    ones = jnp.ones((LANES, LANES), bf16)
    r, c = iota((TILES, TILES), 0), iota((TILES, TILES), 1)
    earlier = jnp.where((c < r) & (r // 4 == c // 4), 1.0, 0.0).astype(bf16)
    inner = jnp.dot(on.astype(bf16), before, preferred_element_type=f32)
    outer = jnp.dot(earlier, on.astype(bf16), preferred_element_type=f32)
    outer = jnp.dot(outer.astype(bf16), ones, preferred_element_type=f32)
    return jnp.where(mask, inner + outer, -1.0)


def selector(rank_ref, block, wave):
    slot = (iota((SLOTS, LANES), 0) + wave * SLOTS).astype(f32)
    parts = [
        jnp.where(rank_ref[pl.ds(4 * block + j, 1), :] == slot, 1.0, 0.0).astype(f32) for j in range(4)
    ]
    return jnp.concatenate(parts, axis=1).astype(bf16)


def in_three(x):
    high = x.astype(bf16)
    rest = x - high.astype(f32)
    mid = rest.astype(bf16)
    low = (rest - mid.astype(f32)).astype(bf16)
    return jnp.concatenate([high, mid, low], axis=0)


def add_three(y, rows):
    return (y[:rows] + y[rows : 2 * rows]) + y[2 * rows :]


def pack_kernel(wave, meta, table, x_ref, bath_ref, slope_ref, wet_ref, up_ref, down_ref, up_rank, down_rank):
    at = masks(table, meta, bath_ref[...], slope_ref[...], wet_ref[...].astype(f32))
    up_rank[...] = ranks(at(D_LOC * meta[0] + D_LOC)[0])
    down_rank[...] = ranks(at(D_LOC * meta[0])[1])
    rows = D_LOC * F_LOC

    def one(block, carry):
        cells = []
        for j in range(4):
            cells.append(
                jnp.concatenate(
                    [x_ref[pl.ds((4 * block + j) * D_LOC + d, F_LOC, stride=ROWS), :] for d in range(D_LOC)],
                    axis=0,
                )
            )
        parts = in_three(jnp.concatenate(cells, axis=1))
        for rank_ref, out_ref in ((up_rank, up_ref), (down_rank, down_ref)):
            chosen = lax.dot_general(
                parts,
                selector(rank_ref, block, wave),
                (((1,), (1,)), ((), ())),
                preferred_element_type=f32,
            )
            out_ref[:, pl.ds(pl.multiple_of(block * SLOTS, SLOTS), SLOTS)] = add_three(chosen, rows)
        return carry

    lax.fori_loop(0, 8, one, 0)


def peak_kernel(meta, table, bath_ref, below_ref, above_ref, slope_ref, heading_ref, wet_ref, refr_ref, shift_ref, out, turn_row, shift_row, marks):
    wet = wet_ref[...].astype(f32)
    gradient = full_gradient(meta, bath_ref[...], below_ref[...], above_ref[...])
    slope, heading = slope_ref[...], heading_ref[...]
    sin_s, cos_s, sin_h, cos_h = jnp.sin(slope), jnp.cos(slope), jnp.sin(heading), jnp.cos(heading)
    sin_peak = jnp.zeros((TILES, LANES), f32)
    cos_peak = jnp.zeros((TILES, LANES), f32)
    for d in range(DIR // 2):
        sin_a, cos_a = table[SIN_CELL + d], table[COS_CELL + d]
        sin_peak = jnp.maximum(sin_peak, jnp.abs(sin_a * cos_s - cos_a * sin_s))
        cos_peak = jnp.maximum(cos_peak, jnp.abs(cos_a * cos_h + sin_a * sin_h))
    turn_row[...] = jnp.abs(gradient) * wet * sin_peak
    shift_row[...] = wet * cos_peak
    turn = jnp.zeros((8, LANES), f32)
    shift = jnp.zeros((8, LANES), f32)
    for t in range(TILES):
        coef, shift_coef = turn_row[t : t + 1, :], shift_row[t : t + 1, :]
        for k in range(3):
            rows = slice(k * 256 + t * 8, k * 256 + t * 8 + 8)
            turn = jnp.maximum(turn, jnp.abs(refr_ref[rows, :]) * coef)
            shift = jnp.maximum(shift, jnp.abs(shift_ref[rows, :]) * shift_coef)
    at = masks(table, meta, bath_ref[...], slope, wet)
    for i in range(8):
        low, high = at(D_LOC * i)
        marks[2 * i * TILES : (2 * i + 1) * TILES, :] = jnp.where(low, 1.0, 0.0).astype(f32)
        marks[(2 * i + 1) * TILES : (2 * i + 2) * TILES, :] = jnp.where(high, 1.0, 0.0).astype(f32)
    ones = jnp.ones((LANES, LANES), bf16)
    group = jnp.where(iota((LANES, 4 * LANES), 0) == iota((LANES, 4 * LANES), 1) // 4, 1.0, 0.0).astype(bf16)
    per_block = jnp.dot(group, marks[...].astype(bf16), preferred_element_type=f32)
    per_block = jnp.dot(per_block.astype(bf16), ones, preferred_element_type=f32)
    out[0] = jnp.max(turn)
    out[1] = jnp.max(shift)
    out[2] = jnp.max(per_block)
    out[3] = 0.0


def turn_kernel(edge, meta, table, peaks, count, x_ref, bath_ref, below_ref, above_ref, slope_ref, wet_ref, refr_ref, left_ref, right_ref, left_more, right_more, *rest):
    if edge:
        y_ref, rim_ref, low_rank, high_rank, speed, sines, halo_l, halo_r = rest
    else:
        y_ref, low_rank, high_rank, speed, sines, halo_l, halo_r = rest
    wet = wet_ref[...].astype(f32)
    at = masks(table, meta, bath_ref[...], slope_ref[...], wet)
    low_rank[...] = ranks(at(D_LOC * meta[0])[0])
    high_rank[...] = ranks(at(D_LOC * meta[0] + D_LOC)[1])
    scale = 0.5 / (jnp.full((TILES, LANES), peaks[0], f32) + EPSILON)
    gradient = full_gradient(meta, bath_ref[...], below_ref[...], above_ref[...])
    tile_block = iota((TILES, LANES), 0) // 4
    counts = jnp.zeros((TILES, LANES), i32)
    for b in range(8):
        counts = jnp.where(tile_block == b, count[b], counts)
    speed[...] = gradient * wet * scale * COS_HALF / counts.astype(f32)
    slope = slope_ref[...]
    sin_s, cos_s = jnp.sin(slope), jnp.cos(slope)
    faces = D_LOC + 2 * KMAX - 1
    for k in range(faces):
        sines[k * TILES : (k + 1) * TILES, :] = face_sine(table, D_LOC * meta[0] - KMAX + 1 + k, sin_s, cos_s)
    first = 2 * (1 - meta[1]) if edge else meta[1]
    groups = 1 if edge else 2
    rows = D_LOC * groups * 8
    overflow = peaks[2] > SLOTS

    def one(block, carry):
        columns = pl.ds(pl.multiple_of(block * SLOTS, SLOTS), SLOTS)

        def sent(ref):
            return in_three(
                jnp.concatenate(
                    [
                        ref[pl.ds(pl.multiple_of(d * F_LOC + first * 8, 8), groups * 8), columns]
                        for d in range(D_LOC)
                    ],
                    axis=0,
                )
            )

        for rank_ref, ref, more, halo in (
            (low_rank, left_ref, left_more, halo_l),
            (high_rank, right_ref, right_more, halo_r),
        ):
            halo[...] = add_three(
                jnp.dot(sent(ref), selector(rank_ref, block, 0), preferred_element_type=f32), rows
            )

            @pl.when(overflow)
            def _():
                halo[...] += add_three(
                    jnp.dot(sent(more), selector(rank_ref, block, 1), preferred_element_type=f32), rows
                )

        steps = count[block]
        for kmax in range(1, KMAX + 1):

            @pl.when(steps == kmax)
            def _():
                for j in range(4):
                    tile = 4 * block + j
                    lanes = slice(j * LANES, (j + 1) * LANES)
                    drive = speed[pl.ds(tile, 1), :]
                    sine = {
                        k: sines[pl.ds(k * TILES + tile, 1), :]
                        for k in range(KMAX - kmax, faces - (KMAX - kmax))
                    }
                    for g in range(groups):
                        group = first + g
                        base = refr_ref[pl.ds(pl.multiple_of(group * 256 + tile * 8, 8), 8), :] * drive
                        cells = []
                        for c in range(KMAX - kmax, D_LOC + KMAX + kmax):
                            d = c % D_LOC
                            at_row = d * groups * 8 + g * 8
                            if c < KMAX:
                                cells.append(halo_l[at_row : at_row + 8, lanes])
                            elif c < KMAX + D_LOC:
                                cells.append(x_ref[pl.ds(group * 8 * ROWS + tile * D_LOC + d, 8, stride=ROWS), :])
                            else:
                                cells.append(halo_r[at_row : at_row + 8, lanes])
                        face = [base * sine[k] for k in sorted(sine)]
                        plus = [jnp.maximum(v, 0.0) for v in face]
                        minus = [jnp.minimum(v, 0.0) for v in face]
                        for step in range(kmax):
                            n = len(cells) - 1
                            flux = [
                                plus[step + i] * cells[i] + minus[step + i] * cells[i + 1] for i in range(n)
                            ]
                            cells = [cells[i + 1] - (flux[i + 1] - flux[i]) for i in range(n - 1)]
                        for d in range(D_LOC):
                            y_ref[pl.ds(g * 8 * ROWS + tile * D_LOC + d, 8, stride=ROWS), :] = cells[d]

        return carry

    lax.fori_loop(0, 8, one, 0)
    if edge:
        for m in range(KMAX):
            row = jnp.where(meta[1] == 0, 7 - m, m)
            rim_ref[m * ROWS : (m + 1) * ROWS, :] = y_ref[pl.ds(pl.multiple_of(row * ROWS, ROWS), ROWS), :]


def shift_kernel(meta, table, peaks, count, near_ref, far_ref, rim_ref, shift_ref, shift_rim_ref, heading_ref, wet_ref, out_ref, sines, cosines, speed):
    wet = wet_ref[...].astype(f32)
    scale = 0.5 / (jnp.full((TILES, LANES), peaks[1], f32) + EPSILON)
    tile_block = iota((TILES, LANES), 0) // 4
    counts = jnp.zeros((TILES, LANES), i32)
    for b in range(8):
        counts = jnp.where(tile_block == b, count[b], counts)
    heading = heading_ref[...]
    sines[...] = jnp.sin(heading)
    cosines[...] = jnp.cos(heading)
    lower = meta[1] == 0
    sign = jnp.where(lower, 0.5, -0.5)
    speed[...] = wet * scale * sign / counts.astype(f32)
    row = iota((8, LANES), 0)
    sin_a = jnp.zeros((8, LANES), f32)
    cos_a = jnp.zeros((8, LANES), f32)
    for d in range(D_LOC):
        here = row % D_LOC == d
        sin_a = jnp.where(here, table[SIN_CELL + D_LOC * meta[0] + d], sin_a)
        cos_a = jnp.where(here, table[COS_CELL + D_LOC * meta[0] + d], cos_a)
    upper_rows = row < D_LOC

    def spread(ref, first, second):
        return jnp.where(upper_rows, ref[pl.ds(first, 1), :], ref[pl.ds(second, 1), :])

    def one(pair, carry):
        tile = 2 * pair
        offset = pl.multiple_of(pair * 8, 8)
        wave = cos_a * spread(cosines, tile, tile + 1) + sin_a * spread(sines, tile, tile + 1)
        drive = wave * spread(speed, tile, tile + 1)
        forward = drive > 0.0
        mask_wet = spread_wet(pair)

        def freq(g):
            return jnp.where(lower, g, F_LOC - 1 - g)

        def coefficient(g):
            f = freq(g)
            at = (f // 8) * 256 + lax.rem(f, 8)
            return spread(shift_ref, at + tile * 8, at + tile * 8 + 8)

        def rim_coefficient(m):
            at = jnp.where(lower, m, 7 - m)
            return spread(shift_rim_ref, at + tile * 8, at + tile * 8 + 8)

        steps = count[pair // 2]
        for kmax in range(1, KMAX + 1):

            @pl.when(steps == kmax)
            def _():
                cells, coefs = [], []
                for g in range(F_LOC):
                    coefs.append(coefficient(g))
                    if g < 16:
                        at = jnp.where(lower, g, 15 - g)
                        cells.append(far_ref[pl.ds(pl.multiple_of(at * ROWS + offset, 8), 8), :])
                    else:
                        at = jnp.where(lower, g - 16, 23 - g)
                        cells.append(near_ref[pl.ds(pl.multiple_of(at * ROWS + offset, 8), 8), :])
                for m in range(kmax):
                    coefs.append(rim_coefficient(m))
                    cells.append(rim_ref[pl.ds(pl.multiple_of(m * ROWS + offset, 8), 8), :])
                face = [(coefs[i] + coefs[i + 1]) * drive for i in range(len(coefs) - 1)]
                for _step in range(kmax):
                    n = len(cells)
                    flux = [face[i] * jnp.where(forward, cells[i], cells[i + 1]) for i in range(n - 1)]
                    cells = [cells[0] - flux[0]] + [cells[i] - (flux[i] - flux[i - 1]) for i in range(1, n - 1)]
                for g in range(F_LOC):
                    out_ref[pl.ds(pl.multiple_of(freq(g) * ROWS + offset, 8), 8), :] = cells[g] * mask_wet

        return carry

    def spread_wet(pair):
        return spread(wets, 2 * pair, 2 * pair + 1)

    wets = Wet(wet_ref)
    lax.fori_loop(0, TILES // 2, one, 0)


class Wet:
    def __init__(self, ref):
        self.ref = ref

    def __getitem__(self, index):
        return self.ref[index].astype(f32)


SMEM = pl.BlockSpec(memory_space=pltpu.SMEM)
VMEM = pl.BlockSpec(memory_space=pltpu.VMEM)


def call(body, outs, in_specs, scratch, flops, moved, args, out_specs=None):
    return pl.pallas_call(
        body,
        out_shape=outs,
        in_specs=in_specs,
        out_specs=out_specs if out_specs is not None else [VMEM] * len(outs),
        scratch_shapes=scratch,
        compiler_params=pltpu.CompilerParams(vmem_limit_bytes=VMEM_LIMIT),
        cost_estimate=pl.CostEstimate(flops=flops, bytes_accessed=moved, transcendentals=0),
    )(*args)


def shape(*dims):
    return jax.ShapeDtypeStruct(dims, f32)


def local(action, bathymetry, refraction, shifting, heading, slope_angle, wet_mask, substeps):
    pts = lax.axis_index(("pts_0", "pts_1"))
    dir_index, freq_index = lax.axis_index("dir"), lax.axis_index("freq")
    meta = jnp.stack([dir_index, freq_index, pts, pts]).astype(i32)
    table = jnp.asarray(angle_table())
    x = action.reshape(F_LOC, D_LOC, TILES, LANES).transpose(0, 2, 1, 3).reshape(F_LOC * ROWS, LANES)
    bath, head, slope, wet = (
        a.reshape(TILES, LANES) for a in (bathymetry, heading, slope_angle, wet_mask)
    )

    def by_eight(a):
        return a.reshape(3, 8, TILES, LANES).transpose(0, 2, 1, 3).reshape(3 * TILES * 8, LANES)

    refr, shift = by_eight(refraction), by_eight(shifting)

    def ring(axis, by):
        count = lax.axis_size(axis)
        return [(i, (i + by) % count) for i in range(count)]

    pts_axes = ("pts_0", "pts_1")
    below = lax.ppermute(bath, pts_axes, ring(pts_axes, 1))
    above = lax.ppermute(bath, pts_axes, ring(pts_axes, -1))

    packed = [shape(D_LOC * F_LOC, 8 * SLOTS)] * 2
    rank = pltpu.VMEM((TILES, LANES), f32)

    def exchange(wave):
        up, down = call(
            functools.partial(pack_kernel, wave),
            packed,
            [SMEM, SMEM] + [VMEM] * 4,
            [rank, rank],
            10**9,
            4 * 10**6,
            (meta, table, x, bath, slope, wet),
        )
        return lax.ppermute(up, "dir", ring("dir", 1)), lax.ppermute(down, "dir", ring("dir", -1))

    left, right = exchange(0)

    rim_group = lax.dynamic_slice(shift, (2 * (1 - freq_index) * 256, 0), (256, LANES))
    swap = [(0, 1), (1, 0)]
    shift_rim = lax.ppermute(rim_group, "freq", swap)

    (local_peaks,) = call(
        peak_kernel,
        [shape(4)],
        [SMEM, SMEM] + [VMEM] * 8,
        [rank, rank, pltpu.VMEM((16 * TILES, LANES), f32)],
        10**7,
        10**6,
        (meta, table, bath, below, above, slope, head, wet, refr, shift),
        out_specs=[SMEM],
    )
    peaks = local_peaks
    for axis in ("pts_0", "pts_1", "freq"):
        peaks = lax.pmax(peaks, axis)

    left_more, right_more = lax.cond(
        peaks[2] > SLOTS,
        lambda: exchange(1),
        lambda: (jnp.zeros((D_LOC * F_LOC, 8 * SLOTS), f32), jnp.zeros((D_LOC * F_LOC, 8 * SLOTS), f32)),
    )

    def turn(edge):
        groups = 1 if edge else 2
        outs = [shape(groups * 8 * ROWS, LANES)] + ([shape(KMAX * ROWS, LANES)] if edge else [])
        halo = pltpu.VMEM((D_LOC * groups * 8, BLK), f32)
        return call(
            functools.partial(turn_kernel, edge),
            outs,
            [SMEM] * 4 + [VMEM] * 11,
            [rank, rank, rank, pltpu.VMEM(((D_LOC + 2 * KMAX - 1) * TILES, LANES), f32), halo, halo],
            10**8,
            4 * 10**6,
            (meta, table, peaks, substeps, x, bath, below, above, slope, wet, refr, left, right, left_more, right_more),
        )

    near, rim = turn(True)
    other_rim = lax.ppermute(rim, "freq", swap)
    (far,) = turn(False)
    (out,) = call(
        shift_kernel,
        [shape(F_LOC * ROWS, LANES)],
        [SMEM] * 4 + [VMEM] * 7,
        [rank, rank, rank],
        10**8,
        4 * 10**6,
        (meta, table, peaks, substeps, near, far, other_rim, shift, shift_rim, head, wet),
    )
    return out.reshape(F_LOC, TILES, D_LOC, LANES).transpose(0, 2, 1, 3).reshape(F_LOC, D_LOC, TILES * LANES)


PTS = ("pts_0", "pts_1")


def solution(mesh):
    torus = Mesh(
        mesh.devices.reshape(8, 2, mesh.shape["dir"], mesh.shape["freq"]),
        ("pts_0", "pts_1", "dir", "freq"),
    )
    in_specs = (
        P("freq", "dir", PTS),
        P(PTS),
        P("freq", PTS),
        P("freq", PTS),
        P(PTS),
        P(PTS),
        P(PTS),
        P(PTS),
    )
    return jax.shard_map(local, mesh=torus, in_specs=in_specs, out_specs=P("freq", "dir", PTS), check_vma=False)
```

time: 157 us -> 84.3 us (0.54)
  other arithmetic: 47.4 us -> 0.08 us
  Pallas kernels: 0 us -> 26.4 us
  waiting for transfers between devices: 19.1 us -> 1.45 us
  blocking collectives: 45 us -> 29.8 us
  starting transfers between devices: 37.7 us -> 22.6 us
  between operations: 4.38 us -> 0.72 us
    pallas_call x0 -> x5, Pallas kernels: none -> 26.4 us  [call(): pl.pallas_call(body, out_shape=outs, in_specs=in_specs, out_specs=out_spe...]
    ppermute x14 -> x6, waiting for transfers between devices: 19.1 us -> 1.45 us  [the longest x1 1.42 us: local(): below = lax.ppermute(bath, pts_axes, ring(pts_axes, 1))]
    add x9 -> x0, other arithmetic: 16.6 us -> none  [the longest x8 16 us: sweep(): jnp.maximum(interface, 0.0) * lower_cells]
    pmax x3, blocking collectives: 45 us -> 29.8 us  [local(): peaks = lax.pmax(peaks, axis)]
    ppermute x14 -> x6, starting transfers between devices: 37.7 us -> 22.6 us  [the longest x1 8.97 us: exchange(): lax.ppermute(down, 'dir', ring('dir', -1))]
    select_n x7 -> x0, other arithmetic: 10.5 us -> none  [sweep(): return jnp.where(active, inner_cells - change, inner_cells)]
    reduce_max x2 -> x0, other arithmetic: 8.8 us -> none  [the longest x1 8.03 us: local(): jnp.max(jnp.abs(jnp.cos(all_angles[:, None] - heading[None, :])), axis=0)]
    mul x6 -> x0, other arithmetic: 2.66 us -> none  [the longest x1 1.69 us: local(): return spectrum * wet_float[None, None, :]]
  transfers between devices with their start and end apart: 14 -> 6, of which waited for: 8 -> 1; matrix products, arithmetic and copies ran while one was open for 25% -> 3% of each run, Pallas kernels for 0% -> 11%
where the time goes in v1:
time: 84.3 us; the launch traced here: 83.7 us
  blocking collectives  29.8 us (35%)
  Pallas kernels  26.4 us (31%)
  starting transfers between devices  22.6 us (27%)
  local copies, waits for them, and re-layouts  2.55 us (3%)
  waiting for transfers between devices  1.45 us (2%)
    pmax x3, blocking collectives, local(): peaks = lax.pmax(peaks, axis)  29.8 us
    pallas_call x5, Pallas kernels, call(): pl.pallas_call(body, out_shape=outs, in_specs=in_specs, out_specs=out_spe...  26.4 us
    ppermute x1, starting transfers between devices, exchange(): lax.ppermute(down, 'dir', ring('dir', -1))  8.97 us
    ppermute x1, starting transfers between devices, exchange(): lax.ppermute(up, 'dir', ring('dir', 1))  6.08 us
    ppermute x1, starting transfers between devices, local(): shift_rim = lax.ppermute(rim_group, 'freq', swap)  3.92 us
    another operation x2, local copies, waits for them, and re-layouts  1.94 us
    ppermute x1, starting transfers between devices, local(): other_rim = lax.ppermute(rim, 'freq', swap)  1.92 us
    ppermute x1, starting transfers between devices, local(): above = lax.ppermute(bath, pts_axes, ring(pts_axes, -1))  1.73 us
  transfers between devices with their start and end apart: 6, of which 1 were waited for; matrix products, arithmetic and copies ran while one was open for 3% of the time, Pallas kernels for 11%

profile of v1, /device:TPU:56, one launch (start us, length us, event | category | flops | bytes accessed | tf_op | source)
XLA Modules:
  0.0 83.7 jit_solution(12767922749313811867)
XLA Ops:
  0.0 0.1 pad_add_fusion.meta
  0.1 0.0 copy-start.5
  0.1 0.0 copy-start
  0.1 0.0 copy-start.1
  0.1 0.0 copy-start.2
  0.1 0.0 copy-start.4
  0.1 0.0 copy-start.6
  0.1 0.0 copy-start.7
  0.1 6.0 %shard_map.92 = (f32[96,2048]{1,0:T(8,128)}, f32[96,2048]{1,0:T(8,128)}) custom-call(s32[4]{0:T(128)S(1)} %pad_add_fusion.meta, f32[256]{0:T(256)} %constant.36.clone.table, f32[3072,128]{1,0:T(8,128)} %bitcast.36, f32[32,128]{1,0:T(8,128)} %bitcast.46, f32[32,128]{1,0:T(8,128)} %bitcast.53, s32[32,128]{1,0:T(8,128)} %bitcast.40), custom_call_target="tpu_custom_call" | custom-call | flops 1000000000 | bytes 4000000 | tf_op jit(solution)/shard_map/pallas_call | solution.py:379
  6.1 6.1 %collective-permute-start.4 = (f32[96,2048]{1,0:T(8,128)}, f32[96,2048]{1,0:T(8,128)S(1)}, u32[]{:S(2)}, u32[]{:S(2)}) collective-permute-start(f32[96,2048]{1,0:T(8,128)} %get-tuple-element.31), channel_id=1, source_target_pairs={{0,2},{2,4},{4,6},{6,8},{8,10},{10,12},{12,14},{14,16},{16,18},{18... | collective-permute-start | bytes 2359304 | tf_op jit(solution)/shard_map/ppermute | solution.py:430
  12.2 9.0 %collective-permute-start.5 = (f32[96,2048]{1,0:T(8,128)}, f32[96,2048]{1,0:T(8,128)S(1)}, u32[]{:S(2)}, u32[]{:S(2)}) collective-permute-start(f32[96,2048]{1,0:T(8,128)} %get-tuple-element.32), channel_id=1, source_target_pairs={{0,30},{2,0},{4,2},{6,4},{8,6},{10,8},{12,10},{14,12},{16,14},{18,... | collective-permute-start | bytes 2359304 | tf_op jit(solution)/shard_map/ppermute | solution.py:430
  21.2 0.0 copy-done.5
  21.2 0.0 collective-permute-start.2
  21.2 1.7 %collective-permute-start.3 = (f32[32,128]{1,0:T(8,128)S(1)}, f32[32,128]{1,0:T(8,128)S(1)}, u32[]{:S(2)}, u32[]{:S(2)}) collective-permute-start(f32[32,128]{1,0:T(8,128)S(1)} %bitcast.48), channel_id=1, source_target_pairs={{0,480},{32,0},{64,32},{96,64},{128,96},{160,128},{192,160},{224,1... | collective-permute-start | bytes 49160 | tf_op jit(solution)/shard_map/ppermute | solution.py:415
  22.9 1.4 %collective-permute-done.2.below_ref = f32[32,128]{1,0:T(8,128)S(1)} collective-permute-done((f32[32,128]{1,0:T(8,128)S(1)}, f32[32,128]{1,0:T(8,128)S(1)}, u32[]{:S(2)}, u32[]{:S(2)}) %collective-permute-start.2) | collective-permute-done | bytes 16416 | tf_op jit(solution)/shard_map/ppermute | solution.py:414
  24.4 0.0 collective-permute-done.3.above_ref
  24.4 0.0 copy-done
  24.4 0.0 copy-done.1
  24.4 0.0 copy-done.2
  24.4 0.0 copy-done.4
  24.4 0.0 copy-done.6
  24.4 0.0 copy-done.7
  24.4 1.9 %shard_map.91 = f32[4]{0:T(128)S(1)} custom-call(s32[4]{0:T(128)S(1)} %pad_add_fusion.meta, f32[256]{0:T(256)S(1)} %copy-done.7, f32[32,128]{1,0:T(8,128)S(1)} %bitcast.49, f32[32,128]{1,0:T(8,128)S(1)} %collective-permute-done.2.below_ref, f32[32,128]{1,0:T(8,128)S(1)} %collective-permute-done.3.above_ref, f32[32,128]{1,0:T(8,128)S(1)} %bitcast.54, ...), custom_call_target="tpu_custom_call" | custom-call | flops 10000000 | bytes 1000000 | tf_op jit(solution)/shard_map/pallas_call | solution.py:379
  26.3 16.2 %pmax.21 = f32[4]{0:T(128)S(1)} all-reduce(f32[4]{0:T(128)S(1)} %shard_map.91), channel_id=1, replica_groups=mesh['pts_0'=8,'pts_1'=2,'dir'=16,'freq'=2] {'pts_0'}, use_global_device_ids=true, to_apply=%region_0.0 | all-reduce | flops 4 | bytes 32 | tf_op jit(solution)/shard_map/pmax | solution.py:450
  42.4 2.5 %pmax.22 = f32[4]{0:T(128)S(1)} all-reduce(f32[4]{0:T(128)S(1)} %pmax.21), channel_id=1, replica_groups=mesh['pts_0'=8,'pts_1'=2,'dir'=16,'freq'=2] {'pts_1'}, use_global_device_ids=true, to_apply=%region_1.0 | all-reduce | flops 4 | bytes 32 | tf_op jit(solution)/shard_map/pmax | solution.py:450
  44.9 11.2 %pmax.23.peaks = f32[4]{0:T(128)S(1)} all-reduce(f32[4]{0:T(128)S(1)} %pmax.22), channel_id=1, replica_groups=mesh['pts_0'=8,'pts_1'=2,'dir'=16,'freq'=2] {'freq'}, use_global_device_ids=true, to_apply=%region_2.0 | all-reduce | flops 4 | bytes 32 | tf_op jit(solution)/shard_map/pmax | solution.py:450
  56.1 0.6 slice.3
  57.2 0.0 copy-start.3
  57.2 1.9 %conditional.1 = (f32[96,2048]{1,0:T(8,128)}, f32[96,2048]{1,0:T(8,128)}) conditional(s32[]{:T(128)} %bitcast.20, () %tuple.13, (s32[4]{0:T(128)S(1)}, f32[256]{0:T(256)S(1)}, f32[3072,128]{1,0:T(8,128)}, f32[32,128]{1,0:T(8,128)S(1)}, f32[32,128]{1,0:T(8,128)S(1)}, /*index=5*/s32[32,128]{1,0:T(8,128)S(1)}) %tuple.21), branch_computations={%region_3.0_spmd, %region_4.0_spmd} | conditional | flops 1000000000 | bytes 10291552 | solution.py:452
  57.3 1.0 %broadcast.2 = f32[96,2048]{1,0:T(8,128)} broadcast(f32[]{:T(128)} %constant.10.clone), dimensions={} | broadcast | bytes 786436 | tf_op jit(solution)/shard_map/broadcast.1
  58.2 1.0 %broadcast.2.clone = f32[96,2048]{1,0:T(8,128)} broadcast(f32[]{:T(128)} %constant.10.clone), dimensions={} | broadcast | bytes 786436 | tf_op jit(solution)/shard_map/broadcast.1
  59.2 0.0 collective-permute-done.4.left_ref
  59.2 0.0 collective-permute-done.5.right_ref
  59.2 0.0 copy-done.3
  59.2 6.2 %shard_map.93 = (f32[1024,128]{1,0:T(8,128)S(1)}, f32[512,128]{1,0:T(8,128)S(1)}) custom-call(s32[4]{0:T(128)S(1)} %pad_add_fusion.meta, f32[256]{0:T(256)S(1)} %copy-done.7, f32[4]{0:T(128)S(1)} %pmax.23.peaks, s32[8]{0:T(128)S(1)} %copy-done.3, f32[3072,128]{1,0:T(8,128)} %bitcast.38, f32[32,128]{1,0:T(8,128)S(1)} %bitcast.51, ...), custom_call_target="tpu_custom_call" | custom-call | flops 100000000 | bytes 4000000 | tf_op jit(solution)/shard_map/pallas_call | solution.py:379
  65.4 1.9 %collective-permute-start.6 = (f32[512,128]{1,0:T(8,128)S(1)}, f32[512,128]{1,0:T(8,128)S(1)}, u32[]{:S(2)}, u32[]{:S(2)}) collective-permute-start(f32[512,128]{1,0:T(8,128)S(1)} %get-tuple-element.36), channel_id=1, source_target_pairs={{0,1},{1,0},{2,3},{3,2},{4,5},{5,4},{6,7},{7,6},{8,9},{9,8},{10,11... | collective-permute-start | bytes 786440 | tf_op jit(solution)/shard_map/ppermute | solution.py:473
  67.4 3.9 %collective-permute-start.7 = (f32[256,128]{1,0:T(8,128)S(1)}, f32[256,128]{1,0:T(8,128)S(1)}, u32[]{:S(2)}, u32[]{:S(2)}) collective-permute-start(f32[256,128]{1,0:T(8,128)S(1)} %constant_dynamic-slice_fusion), channel_id=1, source_target_pairs={{0,1},{1,0},{2,3},{3,2},{4,5},{5,4},{6,7},{7,6},{8,9},{9,8},{10,11... | collective-permute-start | bytes 393224 | tf_op jit(solution)/shard_map/ppermute | solution.py:436
  71.3 7.4 %shard_map.94.far_ref = f32[2048,128]{1,0:T(8,128)S(1)} custom-call(s32[4]{0:T(128)S(1)} %pad_add_fusion.meta, f32[256]{0:T(256)S(1)} %copy-done.7, f32[4]{0:T(128)S(1)} %pmax.23.peaks, s32[8]{0:T(128)S(1)} %copy-done.3, f32[3072,128]{1,0:T(8,128)} %bitcast.39, f32[32,128]{1,0:T(8,128)S(1)} %bitcast.52, f32[32,128]{1,0:T(8,128)S(1)} %collective-permute-done.2.below_ref, ...), custom_call_target="tpu_custom_call" | custom-call | flops 100000000 | bytes 4000000 | tf_op jit(solution)/shard_map/pallas_call | solution.py:379
  78.7 0.0 collective-permute-done.7.shift_rim_ref
  78.7 0.0 collective-permute-done.6.rim_ref
  78.7 5.0 %shard_map.95 = f32[3072,128]{1,0:T(8,128)} custom-call(s32[4]{0:T(128)S(1)} %pad_add_fusion.meta, f32[256]{0:T(256)S(1)} %copy-done.7, f32[4]{0:T(128)S(1)} %pmax.23.peaks, s32[8]{0:T(128)S(1)} %copy-done.3, f32[1024,128]{1,0:T(8,128)S(1)} %get-tuple-element.35.near_ref, f32[2048,128]{1,0:T(8,128)S(1)} %shard_map.94.far_ref, ...), custom_call_target="tpu_custom_call" | custom-call | flops 100000000 | bytes 4000000 | tf_op jit(solution)/shard_map/pallas_call | solution.py:379
  (1 shorter events, 0.0 us)
Async XLA Ops:
  0.1 21.1 %copy-start.5 = (f32[4096]{0:T(1024)S(1)}, f32[4096]{0:T(1024)}, u32[]{:S(2)}) copy-start(f32[4096]{0:T(1024)} %param.12) | copy-start | bytes 49156
  0.1 24.3 %copy-start = (f32[24,4096]{1,0:T(8,128)S(1)}, f32[24,4096]{1,0:T(8,128)}, u32[]{:S(2)}) copy-start(f32[24,4096]{1,0:T(8,128)} %param.13) | copy-start | bytes 1179652
  0.1 24.3 %copy-start.1 = (f32[24,4096]{1,0:T(8,128)S(1)}, f32[24,4096]{1,0:T(8,128)}, u32[]{:S(2)}) copy-start(f32[24,4096]{1,0:T(8,128)} %param.14) | copy-start | bytes 1179652
  0.1 24.3 %copy-start.2 = (f32[4096]{0:T(1024)S(1)}, f32[4096]{0:T(1024)}, u32[]{:S(2)}) copy-start(f32[4096]{0:T(1024)} %param.15) | copy-start | bytes 49156
  0.1 24.3 %copy-start.4 = (s32[4096]{0:T(1024)S(1)}, s32[4096]{0:T(1024)}, u32[]{:S(2)}) copy-start(s32[4096]{0:T(1024)} %param.17) | copy-start | bytes 49156
  0.1 24.3 %copy-start.6 = (f32[4096]{0:T(1024)S(1)}, f32[4096]{0:T(1024)}, u32[]{:S(2)}) copy-start(f32[4096]{0:T(1024)} %param.16) | copy-start | bytes 49156
  0.1 24.3 %copy-start.7 = (f32[256]{0:T(256)S(1)}, f32[256]{0:T(256)}, u32[]{:S(2)}) copy-start(f32[256]{0:T(256)} %constant.36.clone.table) | copy-start | bytes 3076
  6.1 53.1 %collective-permute-start.4 = (f32[96,2048]{1,0:T(8,128)}, f32[96,2048]{1,0:T(8,128)S(1)}, u32[]{:S(2)}, u32[]{:S(2)}) collective-permute-start(f32[96,2048]{1,0:T(8,128)} %get-tuple-element.31), channel_id=1, source_target_pairs={{0,2},{2,4},{4,6},{6,8},{8,10},{10,12},{12,14},{14,16},{16,18},{18... | collective-permute-start | bytes 2359304 | tf_op jit(solution)/shard_map/ppermute | solution.py:430
  12.2 47.0 %collective-permute-start.5 = (f32[96,2048]{1,0:T(8,128)}, f32[96,2048]{1,0:T(8,128)S(1)}, u32[]{:S(2)}, u32[]{:S(2)}) collective-permute-start(f32[96,2048]{1,0:T(8,128)} %get-tuple-element.32), channel_id=1, source_target_pairs={{0,30},{2,0},{4,2},{6,4},{8,6},{10,8},{12,10},{14,12},{16,14},{18,... | collective-permute-start | bytes 2359304 | tf_op jit(solution)/shard_map/ppermute | solution.py:430
  21.2 3.2 %collective-permute-start.2 = (f32[32,128]{1,0:T(8,128)S(1)}, f32[32,128]{1,0:T(8,128)S(1)}, u32[]{:S(2)}, u32[]{:S(2)}) collective-permute-start(f32[32,128]{1,0:T(8,128)S(1)} %bitcast.47), channel_id=1, source_target_pairs={{0,32},{32,64},{64,96},{96,128},{128,160},{160,192},{192,224},{224... | collective-permute-start | bytes 49160 | tf_op jit(solution)/shard_map/ppermute | solution.py:414
  21.2 3.2 %collective-permute-start.3 = (f32[32,128]{1,0:T(8,128)S(1)}, f32[32,128]{1,0:T(8,128)S(1)}, u32[]{:S(2)}, u32[]{:S(2)}) collective-permute-start(f32[32,128]{1,0:T(8,128)S(1)} %bitcast.48), channel_id=1, source_target_pairs={{0,480},{32,0},{64,32},{96,64},{128,96},{160,128},{192,160},{224,1... | collective-permute-start | bytes 49160 | tf_op jit(solution)/shard_map/ppermute | solution.py:415
  57.2 2.0 %copy-start.3 = (s32[8]{0:T(128)S(1)}, s32[8]{0:T(128)}, u32[]{:S(2)}) copy-start(s32[8]{0:T(128)} %count.5) | copy-start | bytes 100
  65.4 13.3 %collective-permute-start.6 = (f32[512,128]{1,0:T(8,128)S(1)}, f32[512,128]{1,0:T(8,128)S(1)}, u32[]{:S(2)}, u32[]{:S(2)}) collective-permute-start(f32[512,128]{1,0:T(8,128)S(1)} %get-tuple-element.36), channel_id=1, source_target_pairs={{0,1},{1,0},{2,3},{3,2},{4,5},{5,4},{6,7},{7,6},{8,9},{9,8},{10,11... | collective-permute-start | bytes 786440 | tf_op jit(solution)/shard_map/ppermute | solution.py:473
  67.4 11.3 %collective-permute-start.7 = (f32[256,128]{1,0:T(8,128)S(1)}, f32[256,128]{1,0:T(8,128)S(1)}, u32[]{:S(2)}, u32[]{:S(2)}) collective-permute-start(f32[256,128]{1,0:T(8,128)S(1)} %constant_dynamic-slice_fusion), channel_id=1, source_target_pairs={{0,1},{1,0},{2,3},{3,2},{4,5},{5,4},{6,7},{7,6},{8,9},{9,8},{10,11... | collective-permute-start | bytes 393224 | tf_op jit(solution)/shard_map/ppermute | solution.py:436

commit v2 on v1

v2 whole, which is shorter than its diff:
```python
import functools
import math

import jax
import jax.numpy as jnp
import numpy as np
from jax import lax
from jax.experimental import pallas as pl
from jax.experimental.pallas import tpu as pltpu
from jax.sharding import Mesh
from jax.sharding import PartitionSpec as P

FREQ = 48
DIR = 64
KMAX = 4
BLK = 512
SLOTS = 256
EPSILON = 1e-06
LANES = 128
F_LOC = 24
D_LOC = 4
TILES = 32
ROWS = TILES * D_LOC
VMEM_LIMIT = 24 * 1024 * 1024
LOW = -3.0e38

f32, bf16, i32 = jnp.float32, jnp.bfloat16, jnp.int32


def angle_table():
    step = 2.0 * math.pi / DIR
    half = np.arange(DIR // 2) * step
    centre = (np.arange(DIR // 2) + 0.5) * step
    parts = [np.sin(half), np.cos(half), np.sin(centre), np.cos(centre)]
    return np.concatenate([np.concatenate([p, -p]) for p in parts]).astype(np.float32)


SIN_FACE, COS_FACE, SIN_CELL, COS_CELL = 0, DIR, 2 * DIR, 3 * DIR
COS_HALF = math.cos(math.pi / DIR)
FACES = D_LOC + 2 * KMAX - 1


def iota(shape, dim):
    return lax.broadcasted_iota(i32, shape, dim)


def shifted(bath):
    lane = iota((TILES, LANES), 1)
    left = pltpu.roll(bath, 1, 1)
    left = jnp.where(lane == 0, pltpu.roll(left, 1, 0), left)
    right = pltpu.roll(bath, LANES - 1, 1)
    right = jnp.where(lane == LANES - 1, pltpu.roll(right, TILES - 1, 0), right)
    return left, right


def end_points():
    point = iota((TILES, LANES), 0) * LANES + iota((TILES, LANES), 1)
    return point == 0, point == TILES * LANES - 1


def face_sine(table, face, sin_s, cos_s):
    at = lax.rem(face + DIR, DIR)
    return table[SIN_FACE + at] * cos_s - table[COS_FACE + at] * sin_s


def masks(table, bath, wet, sin_s, cos_s):
    left, right = shifted(bath)
    drive = (right - left) * wet
    first, last = end_points()
    ends = first | last

    def at(face):
        speed = drive * face_sine(table, face, sin_s, cos_s)
        return (speed > 0.0) | ends, (speed < 0.0) | ends

    return at


def ranks(mask):
    on = jnp.where(mask, 1.0, 0.0).astype(f32).astype(bf16)
    row, col = iota((LANES, LANES), 0), iota((LANES, LANES), 1)
    before = jnp.where(row < col, 1.0, 0.0).astype(bf16)
    ones = jnp.ones((LANES, LANES), bf16)
    r, c = iota((TILES, TILES), 0), iota((TILES, TILES), 1)
    earlier = jnp.where((c < r) & (r // 4 == c // 4), 1.0, 0.0).astype(bf16)
    inner = jnp.dot(on, before, preferred_element_type=f32)
    number = jnp.dot(on, ones, preferred_element_type=f32)
    offset = jnp.dot(earlier, on, preferred_element_type=f32)
    offset = jnp.dot(offset.astype(bf16), ones, preferred_element_type=f32)
    return inner.astype(i32), offset.astype(i32), number.astype(i32)


def gather(x, index):
    return jnp.take_along_axis(x, index, axis=1)


def packing(mask, wave, source_ref, slot_ref):
    inner, offset, number = ranks(mask)
    lane = iota((TILES, LANES), 1)
    code = jnp.where(mask, (lane - inner) * 128 + lane + 65536, 0)
    for bit in range(7):
        step = 1 << bit
        far = pltpu.roll(code, LANES - step, 1)
        comes = (far & (128 << bit)) != 0
        goes = (code & (128 << bit)) != 0
        code = jnp.where(comes, far - (128 << bit), jnp.where(goes, 0, code))
    source = gather((code & 127).astype(f32), (lane - offset) & 127)
    source_ref[...] = source.astype(i32)
    slot = lane + ((offset - lane + 127) >> 7) * LANES
    slot_ref[...] = jnp.where(slot < offset + number, slot - wave * SLOTS, -1)


def pack_block(x_ref, block, source, slot, outs):
    for d in range(D_LOC):
        for g in range(3):
            x = [x_ref[pl.ds(g * 8 * ROWS + (4 * block + j) * D_LOC + d, 8, stride=ROWS), :] for j in range(4)]
            for s_ref, k_ref, out in zip(source, slot, outs):
                low = jnp.zeros((8, LANES), f32)
                high = jnp.zeros((8, LANES), f32)
                for j in range(4):
                    tile = pl.ds(4 * block + j, 1)
                    taken = gather(x[j], jnp.broadcast_to(s_ref[tile, :], (8, LANES)))
                    half = jnp.broadcast_to(k_ref[tile, :], (8, LANES)) >> 7
                    low = jnp.where(half == 0, taken, low)
                    high = jnp.where(half == 1, taken, high)
                rows = slice((d * 3 + g) * 8, (d * 3 + g) * 8 + 8)
                out[rows, pl.ds(pl.multiple_of(block * SLOTS, SLOTS), LANES)] = low
                out[rows, pl.ds(pl.multiple_of(block * SLOTS + LANES, LANES), LANES)] = high


def more_kernel(meta, table, x_ref, bath_ref, slope_ref, wet_ref, up_ref, down_ref, *scratch):
    slope = slope_ref[...]
    at = masks(table, bath_ref[...], wet_ref[...].astype(f32), jnp.sin(slope), jnp.cos(slope))
    packing(at(D_LOC * meta[0] + D_LOC)[0], 1, scratch[0], scratch[1])
    packing(at(D_LOC * meta[0])[1], 1, scratch[2], scratch[3])

    def one(block, carry):
        pack_block(x_ref, block, scratch[::2], scratch[1::2], (up_ref, down_ref))
        return carry

    lax.fori_loop(0, 8, one, 0)


def part(edge, meta):
    return (2 * (1 - meta[1]), 1) if edge else (meta[1], 2)


def rows_of(x_hbm, edge, meta):
    first, groups = part(edge, meta)
    return x_hbm.at[pl.ds(pl.multiple_of(first * 8 * ROWS, 8 * ROWS), groups * 8 * ROWS), :]


def fetch(pairs, sems):
    copies = [pltpu.make_async_copy(source, target, sems.at[i]) for i, (source, target) in enumerate(pairs)]
    for copy in copies:
        copy.start()
    return copies


def pack_kernel(meta, table, bath_hbm, slope_hbm, wet_hbm, x_hbm, up_hbm, down_hbm, bath_ref, slope_ref, wet_ref, x_ref, up_ref, down_ref, sems, in_sems, up_sems, down_sems, *scratch):
    def arrival(c):
        rows = pl.ds(pl.multiple_of(c * 8 * D_LOC, 8 * D_LOC), 8 * D_LOC)
        return pltpu.make_async_copy(x_hbm.at[:, rows, :], x_ref.at[:, rows, :], in_sems.at[c])

    def departures(c):
        columns = pl.ds(pl.multiple_of(c * 2 * SLOTS, 2 * SLOTS), 2 * SLOTS)
        return (
            pltpu.make_async_copy(up_ref.at[:, columns], up_hbm.at[:, columns], up_sems.at[c]),
            pltpu.make_async_copy(down_ref.at[:, columns], down_hbm.at[:, columns], down_sems.at[c]),
        )

    copies = fetch(((bath_hbm, bath_ref), (slope_hbm, slope_ref), (wet_hbm, wet_ref)), sems)
    for c in range(4):
        arrival(c).start()
    for copy in copies:
        copy.wait()
    slope = slope_ref[...]
    at = masks(table, bath_ref[...], wet_ref[...].astype(f32), jnp.sin(slope), jnp.cos(slope))
    packing(at(D_LOC * meta[0] + D_LOC)[0], 0, scratch[0], scratch[1])
    packing(at(D_LOC * meta[0])[1], 0, scratch[2], scratch[3])
    flat = x_ref.reshape(F_LOC * ROWS, LANES)

    def two(c, carry):
        arrival(c).wait()
        for block in (2 * c, 2 * c + 1):
            pack_block(flat, block, scratch[::2], scratch[1::2], (up_ref, down_ref))
        for copy in departures(c):
            copy.start()
        return carry

    lax.fori_loop(0, 4, two, 0)
    for c in range(4):
        for copy in departures(c):
            copy.wait()


def note_kernel(meta, table, count, bath_hbm, slope_hbm, wet_hbm, heading_hbm, refr_hbm, shift_hbm, note_ref, halo_ref, sine_ref, wave_ref, shift_rim_ref, bath_ref, slope_ref, wet_ref, heading_ref, refr_ref, shift_ref, sems, turn_row, shift_row, refr_row, marks):
    copies = fetch(
        (
            (bath_hbm, bath_ref),
            (slope_hbm, slope_ref),
            (wet_hbm, wet_ref),
            (heading_hbm, heading_ref),
            (refr_hbm, refr_ref),
            (shift_hbm, shift_ref),
        ),
        sems,
    )
    for copy in copies[:4]:
        copy.wait()
    wet, bath = wet_ref[...].astype(f32), bath_ref[...]
    slope, heading = slope_ref[...], heading_ref[...]
    sin_s, cos_s, sin_h, cos_h = jnp.sin(slope), jnp.cos(slope), jnp.sin(heading), jnp.cos(heading)
    at = masks(table, bath, wet, sin_s, cos_s)
    sin_peak = jnp.zeros((TILES, LANES), f32)
    cos_peak = jnp.zeros((TILES, LANES), f32)
    for d in range(DIR // 2):
        sin_a, cos_a = table[SIN_CELL + d], table[COS_CELL + d]
        sin_peak = jnp.maximum(sin_peak, jnp.abs(sin_a * cos_s - cos_a * sin_s))
        cos_peak = jnp.maximum(cos_peak, jnp.abs(cos_a * cos_h + sin_a * sin_h))
    left, right = shifted(bath)
    first, last = end_points()
    gradient = jnp.where(first | last, 0.0, (right - left) * 0.5)
    turn_row[...] = jnp.abs(gradient) * wet * sin_peak
    shift_row[...] = wet * cos_peak
    turn = jnp.zeros((8, LANES), f32)
    shift = jnp.zeros((8, LANES), f32)
    ends = []
    for copy in copies[4:]:
        copy.wait()
    for t in range(TILES):
        coef, shift_coef = turn_row[t : t + 1, :], shift_row[t : t + 1, :]
        most, most_shift = jnp.zeros((8, LANES), f32), jnp.zeros((8, LANES), f32)
        for k in range(3):
            rows = slice(k * 256 + t * 8, k * 256 + t * 8 + 8)
            most = jnp.maximum(most, jnp.abs(refr_ref[rows, :]))
            most_shift = jnp.maximum(most_shift, jnp.abs(shift_ref[rows, :]))
        turn = jnp.maximum(turn, most * coef)
        shift = jnp.maximum(shift, most_shift * shift_coef)
        if t in (0, TILES - 1):
            ends.append(jnp.max(most, axis=0, keepdims=True))
    for i in range(8):
        low, high = at(D_LOC * i)
        marks[2 * i * TILES : (2 * i + 1) * TILES, :] = jnp.where(low, 1.0, 0.0).astype(f32)
        marks[(2 * i + 1) * TILES : (2 * i + 2) * TILES, :] = jnp.where(high, 1.0, 0.0).astype(f32)
    ones = jnp.ones((LANES, LANES), bf16)
    group = jnp.where(iota((LANES, 4 * LANES), 0) == iota((LANES, 4 * LANES), 1) // 4, 1.0, 0.0).astype(bf16)
    per_block = jnp.dot(group, marks[...].astype(bf16), preferred_element_type=f32)
    per_block = jnp.dot(per_block.astype(bf16), ones, preferred_element_type=f32)

    weight = wet * sin_peak
    row, lane = iota((8, LANES), 0), iota((8, LANES), 1)
    note = jnp.where(row == 0, jnp.where(lane == 0, jnp.max(turn), jnp.max(shift)), LOW)
    note = jnp.where((row == 0) & (lane == 2), jnp.max(per_block), note)
    refr_row[0:1, :] = ends[0] * weight[0:1, :]
    refr_row[1:2, :] = ends[1] * weight[TILES - 1 : TILES, :]
    mine = lane == meta[2]
    for r, value in enumerate(
        (
            bath_ref[0:1, 0:1],
            bath_ref[0:1, 1:2],
            bath_ref[TILES - 1 : TILES, LANES - 2 : LANES - 1],
            bath_ref[TILES - 1 : TILES, LANES - 1 : LANES],
            refr_row[0:1, 0:1],
            refr_row[1:2, LANES - 1 : LANES],
        )
    ):
        note = jnp.where((row == 1 + r) & mine, value, note)
    note_ref[...] = note
    first = 2 * (1 - meta[1])
    for m in range(KMAX):
        row = jnp.where(meta[1] == 0, 7 - m, m)
        shift_rim_ref[m * TILES : (m + 1) * TILES, :] = shift_ref[pl.ds(first * 256 + row, TILES, stride=8), :]

    unpacking(at(D_LOC * meta[0])[0], halo_ref, 0)
    unpacking(at(D_LOC * meta[0] + D_LOC)[1], halo_ref, 2)
    for k in range(FACES):
        sine_ref[k * TILES : (k + 1) * TILES, :] = face_sine(table, D_LOC * meta[0] - KMAX + 1 + k, sin_s, cos_s)
    sign = jnp.where(meta[1] == 0, 0.5, -0.5)
    speed = wet * sign / block_counts(count)
    for d in range(D_LOC):
        sin_a, cos_a = table[SIN_CELL + D_LOC * meta[0] + d], table[COS_CELL + D_LOC * meta[0] + d]
        wave_ref[pl.ds(d, TILES, stride=D_LOC), :] = (cos_a * cos_h + sin_a * sin_h) * speed


def full_gradient(meta, note, bath):
    row, lane = iota((8, LANES), 0), iota((8, LANES), 1)
    below = jnp.max(jnp.where((row == 4) & (lane == meta[2] - 1), note, LOW))
    above = jnp.max(jnp.where((row == 1) & (lane == meta[2] + 1), note, LOW))
    left, right = shifted(bath)
    first, last = end_points()
    left = jnp.where(first, jnp.where(meta[2] == 0, bath, below), left)
    right = jnp.where(last, jnp.where(meta[2] == 15, bath, above), right)
    return (right - left) * 0.5


def largest_turn(note):
    lane = iota((1, LANES), 1)
    first, second, second_last, last = (note[r : r + 1, :] for r in range(1, 5))
    below = jnp.where(lane == 0, first, pltpu.roll(jnp.broadcast_to(last, (8, LANES)), 1, 1)[0:1, :])
    above = jnp.where(lane == 15, last, pltpu.roll(jnp.broadcast_to(first, (8, LANES)), LANES - 1, 1)[0:1, :])
    at_first = jnp.abs(second - below) * 0.5 * note[5:6, :]
    at_last = jnp.abs(above - second_last) * 0.5 * note[6:7, :]
    here = jnp.where(lane < 16, jnp.maximum(at_first, at_last), 0.0)
    return jnp.maximum(jnp.max(here), jnp.max(jnp.where(lane == 0, note[0:1, :], 0.0)))


def block_counts(count):
    tile_block = iota((TILES, LANES), 0) // 4
    counts = jnp.zeros((TILES, LANES), i32)
    for b in range(8):
        counts = jnp.where(tile_block == b, count[b], counts)
    return counts.astype(f32)


def unpacking(mask, ref, at):
    inner, offset, _ = ranks(mask)
    ref[at * TILES : (at + 1) * TILES, :] = (inner + offset) & 127
    ref[(at + 1) * TILES : (at + 2) * TILES, :] = (offset - iota((TILES, LANES), 1) + 127) >> 7


def turn_kernel(edge, meta, count, note_ref, other_ref, x_hbm, bath_ref, wet_ref, refr_ref, halo_ref, sines, left_ref, right_ref, left_hbm, right_hbm, *rest):
    if edge:
        y_ref, rim_ref, *rest = rest
    else:
        y_ref, *rest = rest
    speed, left_more, right_more, x_ref, sems = rest
    (copy,) = fetch(((rows_of(x_hbm, edge, meta), x_ref),), sems)
    note = jnp.maximum(note_ref[...], other_ref[0:8, :])
    scale = 0.5 / (jnp.full((TILES, LANES), largest_turn(note), f32) + EPSILON)
    wet = wet_ref[...].astype(f32)
    speed[...] = full_gradient(meta, note, bath_ref[...]) * wet * scale * COS_HALF / block_counts(count)
    first, groups = part(edge, meta)
    copy.wait()
    overflow = jnp.max(jnp.where(iota((1, LANES), 1) == 2, note[0:1, :], LOW)) > SLOTS

    def halo(wide, d, g, block, refs, tile):
        ref, more, at = refs

        def eight(k):
            return jnp.broadcast_to(halo_ref[pl.ds(k * TILES + tile, 1), :], (8, LANES))

        def slots(source, half, row):
            lanes = pl.ds(pl.multiple_of(block * SLOTS + half * LANES, LANES), LANES)
            return source[pl.ds(pl.multiple_of(row, 8), 8), lanes]

        half = eight(at + 1)
        row = (d * 3 + first + g) * 8
        values = jnp.where(half == 0, slots(ref, 0, row), slots(ref, 1, row))
        if wide:
            values = jnp.where(half == 2, slots(more, 0, row), values)
            values = jnp.where(half == 3, slots(more, 1, row), values)
        return gather(values, eight(at))

    def sweep(wide, block, carry):
        low = (left_ref, left_more, 0)
        high = (right_ref, right_more, 2)
        steps = count[block]
        for kmax in range(1, KMAX + 1):

            @pl.when(steps == kmax)
            def _():
                for j in range(4):
                    tile = 4 * block + j
                    drive = speed[pl.ds(tile, 1), :]
                    sine = [
                        sines[pl.ds(k * TILES + tile, 1), :] for k in range(KMAX - kmax, FACES - (KMAX - kmax))
                    ]
                    for g in range(groups):
                        group = first + g
                        base = refr_ref[pl.ds(pl.multiple_of(group * 256 + tile * 8, 8), 8), :] * drive
                        cells = []
                        for c in range(KMAX - kmax, D_LOC + KMAX + kmax):
                            d = c % D_LOC
                            if c < KMAX:
                                cells.append(halo(wide, d, g, block, low, tile))
                            elif c < KMAX + D_LOC:
                                cells.append(x_ref[pl.ds(g * 8 * ROWS + tile * D_LOC + d, 8, stride=ROWS), :])
                            else:
                                cells.append(halo(wide, d, g, block, high, tile))
                        face = [base * v for v in sine]
                        plus = [jnp.maximum(v, 0.0) for v in face]
                        minus = [jnp.minimum(v, 0.0) for v in face]
                        for step in range(kmax):
                            n = len(cells) - 1
                            flux = [
                                plus[step + i] * cells[i] + minus[step + i] * cells[i + 1] for i in range(n)
                            ]
                            cells = [cells[i + 1] - (flux[i + 1] - flux[i]) for i in range(n - 1)]
                        for d in range(D_LOC):
                            y_ref[pl.ds(g * 8 * ROWS + tile * D_LOC + d, 8, stride=ROWS), :] = cells[d]

        return carry

    @pl.when(overflow)
    def _():
        pltpu.sync_copy(left_hbm, left_more)
        pltpu.sync_copy(right_hbm, right_more)
        lax.fori_loop(0, 8, functools.partial(sweep, True), 0)

    @pl.when(jnp.logical_not(overflow))
    def _():
        lax.fori_loop(0, 8, functools.partial(sweep, False), 0)

    if edge:
        for m in range(KMAX):
            row = jnp.where(meta[1] == 0, 7 - m, m)
            rim_ref[m * ROWS : (m + 1) * ROWS, :] = y_ref[pl.ds(pl.multiple_of(row * ROWS, ROWS), ROWS), :]


def shift_kernel(rim, meta, count, note_ref, other_ref, near_ref, far_ref, shift_ref, wave_ref, wet_ref, *rest):
    if rim:
        rim_ref, _, out_hbm, wets, out_ref, sems = rest
    else:
        out_hbm, wets, out_ref, sems = rest
    note = jnp.maximum(note_ref[0:1, :], other_ref[0:1, :])
    peak = jnp.max(jnp.where(iota((1, LANES), 1) == 1, note, LOW))
    wets[...] = wet_ref[...].astype(f32)
    scale = 0.5 / (jnp.full((8, LANES), peak, f32) + EPSILON)
    upper_rows = iota((8, LANES), 0) < D_LOC

    def spread(ref, first, second):
        return jnp.where(upper_rows, ref[pl.ds(first, 1), :], ref[pl.ds(second, 1), :])

    def one(lower, pair, carry):
        tile = 2 * pair
        offset = pl.multiple_of(pair * 8, 8)
        eights = pl.multiple_of(tile * 8, 8)
        drive = wave_ref[pl.ds(offset, 8), :] * scale
        forward = drive > 0.0
        mask_wet = spread(wets, tile, tile + 1)

        def coefficient(g):
            if g >= F_LOC:
                at = 8 + (g - F_LOC) * TILES + tile
                return spread(other_ref, at, at + 1)
            f = g if lower else F_LOC - 1 - g
            at = (f // 8) * 256 + f % 8 + eights
            return spread(shift_ref, at, at + 8)

        def cell(g):
            if g >= F_LOC:
                ref, row = rim_ref, g - F_LOC
            elif g < 16:
                ref, row = far_ref, (g if lower else 15 - g)
            else:
                ref, row = near_ref, (g - 16 if lower else 23 - g)
            return ref[pl.ds(row * ROWS + offset, 8), :]

        steps = count[pair // 2]
        for kmax in range(1, KMAX + 1):

            @pl.when(steps == kmax)
            def _():
                which = range(16 - kmax, F_LOC + kmax) if rim else range(16 + kmax)
                cells = [cell(g) for g in which]
                coefs = [coefficient(g) for g in which]
                face = [(coefs[i] + coefs[i + 1]) * drive for i in range(len(coefs) - 1)]
                for step in range(kmax):
                    n = len(cells)
                    used = face[step:] if rim else face
                    flux = [used[i] * jnp.where(forward, cells[i], cells[i + 1]) for i in range(n - 1)]
                    inner = [cells[i] - (flux[i] - flux[i - 1]) for i in range(1, n - 1)]
                    cells = inner if rim else [cells[0] - flux[0]] + inner
                count_out = 8 if rim else 16
                for i in range(count_out):
                    row = i if lower else count_out - 1 - i
                    out_ref[pl.ds(row * ROWS + offset, 8), :] = cells[i] * mask_wet

        return carry

    @pl.when(meta[1] == 0)
    def _():
        lax.fori_loop(0, TILES // 2, functools.partial(one, True), 0)

    @pl.when(meta[1] == 1)
    def _():
        lax.fori_loop(0, TILES // 2, functools.partial(one, False), 0)

    (copy,) = fetch(((out_ref, rows_of(out_hbm, rim, meta)),), sems)
    copy.wait()


SMEM = pl.BlockSpec(memory_space=pltpu.SMEM)
VMEM = pl.BlockSpec(memory_space=pltpu.VMEM)
ANY = pl.BlockSpec(memory_space=pl.ANY)
HBM = pl.BlockSpec(memory_space=pltpu.HBM)


def call(body, outs, in_specs, scratch, args, out_specs=None, aliases=None):
    return pl.pallas_call(
        body,
        out_shape=outs,
        in_specs=in_specs,
        out_specs=out_specs if out_specs is not None else [VMEM] * len(outs),
        scratch_shapes=scratch,
        input_output_aliases=aliases or {},
        compiler_params=pltpu.CompilerParams(vmem_limit_bytes=VMEM_LIMIT),
        cost_estimate=pl.CostEstimate(flops=0, bytes_accessed=0, transcendentals=0),
    )(*args)


def in_hbm(*arrays):
    return [pltpu.with_memory_space_constraint(a, pltpu.HBM) for a in arrays]


def shape(*dims):
    return jax.ShapeDtypeStruct(dims, f32)


def local(action, bathymetry, refraction, shifting, heading, slope_angle, wet_mask, substeps):
    pts = lax.axis_index(("pts_0", "pts_1"))
    dir_index, freq_index = lax.axis_index("dir"), lax.axis_index("freq")
    meta = jnp.stack([dir_index, freq_index, pts, pts]).astype(i32)
    table = jnp.asarray(angle_table())
    x = action.reshape(F_LOC, D_LOC, TILES, LANES).transpose(0, 2, 1, 3).reshape(F_LOC * ROWS, LANES)
    bath, head, slope, wet = (
        a.reshape(TILES, LANES) for a in (bathymetry, heading, slope_angle, wet_mask)
    )

    def by_eight(a):
        return a.reshape(3, 8, TILES, LANES).transpose(0, 2, 1, 3).reshape(3 * TILES * 8, LANES)

    refr, shift = by_eight(refraction), by_eight(shifting)
    count = lax.axis_size("dir")
    ring_up = [(i, (i + 1) % count) for i in range(count)]
    ring_down = [((i + 1) % count, i) for i in range(count)]
    swap = [(0, 1), (1, 0)]

    wave = [shape(D_LOC * F_LOC, 8 * SLOTS)] * 2
    row = pltpu.VMEM((TILES, LANES), f32)
    row_int = pltpu.VMEM((TILES, LANES), i32)

    def exchange(up, down):
        return lax.ppermute(up, "dir", ring_up), lax.ppermute(down, "dir", ring_down)

    small = [row, row, row_int]
    coefs = pltpu.VMEM((3 * TILES * 8, LANES), f32)
    dma = pltpu.SemaphoreType.DMA
    packed = pltpu.VMEM((D_LOC * F_LOC, 8 * SLOTS), f32)
    up, down = call(
        pack_kernel,
        wave,
        [SMEM, SMEM] + [HBM] * 4,
        small + [pltpu.VMEM((F_LOC, ROWS, LANES), f32), packed, packed, dma((3,)), dma((4,)), dma((4,)), dma((4,))] + [row_int] * 4,
        (meta, table, *in_hbm(bath, slope, wet, x.reshape(F_LOC, ROWS, LANES))),
        out_specs=[ANY, ANY],
    )
    left, right = exchange(up, down)
    note, halo, sines, waves, shift_rim = call(
        note_kernel,
        [
            shape(8, LANES),
            jax.ShapeDtypeStruct((4 * TILES, LANES), i32),
            shape(FACES * TILES, LANES),
            shape(ROWS, LANES),
            shape(KMAX * TILES, LANES),
        ],
        [SMEM] * 3 + [HBM] * 6,
        small
        + [row, coefs, coefs, dma((6,)), row, row]
        + [pltpu.VMEM((8, LANES), f32), pltpu.VMEM((16 * TILES, LANES), f32)],
        (meta, table, substeps, *in_hbm(bath, slope, wet, head, refr, shift)),
    )
    for axis in ("pts_0", "pts_1"):
        note = lax.pmax(note, axis)
    other = lax.ppermute(jnp.concatenate([note, shift_rim], axis=0), "freq", swap)

    def second_wave():
        return exchange(
            *call(
                more_kernel,
                wave,
                [SMEM, SMEM] + [VMEM] * 4,
                [row_int] * 4,
                (meta, table, x, bath, slope, wet),
            )
        )

    def no_wave():
        return tuple(call(lambda *refs: None, wave, [], [], (), out_specs=[ANY, ANY]))

    left_more, right_more = lax.cond(note[0, 2] > SLOTS, second_wave, no_wave)

    def turn(edge):
        groups = 1 if edge else 2
        outs = [shape(groups * 8 * ROWS, LANES)] + ([shape(KMAX * ROWS, LANES)] if edge else [])
        own = [pltpu.VMEM((groups * 8 * ROWS, LANES), f32), dma((1,))]
        return call(
            functools.partial(turn_kernel, edge),
            outs,
            [SMEM] * 2 + [VMEM] * 2 + [HBM] + [VMEM] * 7 + [ANY] * 2,
            [row, packed, packed] + own,
            (meta, substeps, note, other, *in_hbm(x), bath, wet, refr, halo, sines, left, right, left_more, right_more),
        )

    near, rim = turn(True)
    other_rim = lax.ppermute(rim, "freq", swap)
    (far,) = turn(False)

    def shifted_part(rim, more):
        groups = 1 if rim else 2
        (out,) = call(
            functools.partial(shift_kernel, rim),
            [shape(F_LOC * ROWS, LANES)],
            [SMEM] * 2 + [VMEM] * 7 + [VMEM, ANY][: len(more)],
            [row, pltpu.VMEM((groups * 8 * ROWS, LANES), f32), dma((1,))],
            (meta, substeps, note, other, near, far, shift, waves, wet, *more),
            out_specs=[ANY],
            aliases={10: 0} if rim else None,
        )
        return out

    out = shifted_part(True, (other_rim, shifted_part(False, ())))
    return out.reshape(F_LOC, TILES, D_LOC, LANES).transpose(0, 2, 1, 3).reshape(F_LOC, D_LOC, TILES * LANES)


PTS = ("pts_0", "pts_1")


def solution(mesh):
    torus = Mesh(
        mesh.devices.reshape(8, 2, mesh.shape["dir"], mesh.shape["freq"]),
        ("pts_0", "pts_1", "dir", "freq"),
    )
    in_specs = (
        P("freq", "dir", PTS),
        P(PTS),
        P("freq", PTS),
        P("freq", PTS),
        P(PTS),
        P(PTS),
        P(PTS),
        P(PTS),
    )
    return jax.shard_map(local, mesh=torus, in_specs=in_specs, out_specs=P("freq", "dir", PTS), check_vma=False)
```

time: 84.3 us -> 73.6 us (0.87)
  blocking collectives: 29.8 us -> 17.4 us
  waiting for transfers between devices: 1.45 us -> 12.8 us
  Pallas kernels: 26.4 us -> 20.6 us
  starting transfers between devices: 22.6 us -> 20.6 us
  local copies, waits for them, and re-layouts: 2.55 us -> 0.7 us
    pmax x3 -> x2, blocking collectives: 29.8 us -> 17.4 us  [local(): note = lax.pmax(note, axis)]
    ppermute x5 -> x3, waiting for transfers between devices: 1.45 us -> 11.6 us  [the longest x1 11.6 us: local(): lax.ppermute(jnp.concatenate([note, shift_rim], axis=0), 'freq', swap)]
    pallas_call x5 -> x7, Pallas kernels: 26.4 us -> 20.6 us  [call(): pl.pallas_call(body, out_shape=outs, in_specs=in_specs, out_specs=out_spe...]
    ppermute x5 -> x3, starting transfers between devices: 20.7 us -> 18.6 us  [the longest x1 8.96 us: exchange(): lax.ppermute(down, 'dir', ring_down)]
    another operation x2 -> x0, local copies, waits for them, and re-layouts: 1.94 us -> none
    ppermute x1, waiting for transfers between devices: 0.01 us -> 1.18 us  [local(): other_rim = lax.ppermute(rim, 'freq', swap)]
  transfers between devices with their start and end apart: 6 -> 4, of which waited for: 1 -> 2; matrix products, arithmetic and copies ran while one was open for 3% -> 1% of each run, Pallas kernels for 11% -> 12%
where the time goes in v2:
time: 73.6 us; the launch traced here: 73.1 us
  Pallas kernels  20.6 us (28%)
  starting transfers between devices  20.6 us (28%)
  blocking collectives  17.4 us (24%)
  waiting for transfers between devices  12.8 us (17%)
  between operations  0.9 us (1%)
    pallas_call x7, Pallas kernels, call(): pl.pallas_call(body, out_shape=outs, in_specs=in_specs, out_specs=out_spe...  20.6 us
    pmax x2, blocking collectives, local(): note = lax.pmax(note, axis)  17.4 us
    ppermute x1, waiting for transfers between devices, local(): lax.ppermute(jnp.concatenate([note, shift_rim], axis=0), 'freq', swap)  11.6 us
    ppermute x1, starting transfers between devices, exchange(): lax.ppermute(down, 'dir', ring_down)  8.96 us
    ppermute x1, starting transfers between devices, exchange(): lax.ppermute(up, 'dir', ring_up)  6.22 us
    ppermute x1, starting transfers between devices, local(): lax.ppermute(jnp.concatenate([note, shift_rim], axis=0), 'freq', swap)  3.38 us
    ppermute x1, starting transfers between devices, local(): other_rim = lax.ppermute(rim, 'freq', swap)  2.05 us
  transfers between devices with their start and end apart: 4, of which 2 were waited for; matrix products, arithmetic and copies ran while one was open for 1% of the time, Pallas kernels for 12%

profile of v2, /device:TPU:56, one launch (start us, length us, event | category | flops | bytes accessed | tf_op | source)
XLA Modules:
  0.0 73.1 jit_solution(18033321008389831271)
XLA Ops:
  0.0 0.0 copy-start.10
  0.0 0.0 copy-start.7
  0.0 0.0 copy-start.9
  0.0 0.0 copy-start.8
  0.0 0.0 copy-start.2
  0.0 0.1 pad_add_fusion.meta
  0.1 6.0 %shard_map.92 = (f32[96,2048]{1,0:T(8,128)}, f32[96,2048]{1,0:T(8,128)S(1)}) custom-call(s32[4]{0:T(128)S(1)} %pad_add_fusion.meta, f32[256]{0:T(256)} %constant.25.clone.table, f32[32,128]{1,0:T(8,128)} %bitcast.47, f32[32,128]{1,0:T(8,128)} %bitcast.52, s32[32,128]{1,0:T(8,128)} %bitcast.40, f32[24,128,128]{2,1,0:T(8,128)} %bitcast.36), custom_call_target="tpu_custom_call" | custom-call | tf_op jit(solution)/shard_map/pallas_call | solution.py:491
  6.1 0.0 copy-start.1
  6.2 6.2 %collective-permute-start.3 = (f32[96,2048]{1,0:T(8,128)}, f32[96,2048]{1,0:T(8,128)S(1)}, u32[]{:S(2)}, u32[]{:S(2)}) collective-permute-start(f32[96,2048]{1,0:T(8,128)} %get-tuple-element.40), channel_id=1, source_target_pairs={{0,2},{2,4},{4,6},{6,8},{8,10},{10,12},{12,14},{14,16},{16,18},{18... | collective-permute-start | bytes 2359304 | tf_op jit(solution)/shard_map/ppermute | solution.py:535
  12.4 9.0 %collective-permute-start.4 = (f32[96,2048]{1,0:T(8,128)S(1)}, f32[96,2048]{1,0:T(8,128)S(1)}, u32[]{:S(2)}, u32[]{:S(2)}) collective-permute-start(f32[96,2048]{1,0:T(8,128)S(1)} %get-tuple-element.41), channel_id=1, source_target_pairs={{2,0},{4,2},{6,4},{8,6},{10,8},{12,10},{14,12},{16,14},{18,16},{20... | collective-permute-start | bytes 2359304 | tf_op jit(solution)/shard_map/ppermute | solution.py:535
  21.4 0.0 copy-done.10
  21.4 0.0 copy-done.2
  21.4 2.3 %shard_map.91 = (f32[8,128]{1,0:T(8,128)S(1)}, s32[128,128]{1,0:T(8,128)S(1)}, f32[352,128]{1,0:T(8,128)S(1)}, f32[128,128]{1,0:T(8,128)S(1)}, f32[128,128]{1,0:T(8,128)S(1)}) custom-call(s32[4]{0:T(128)S(1)} %pad_add_fusion.meta, f32[256]{0:T(256)S(1)} %copy-done.10, s32[8]{0:T(128)S(1)} %copy-done.2, f32[32,128]{1,0:T(8,128)} %bitcast.48, ...), custom_call_target="tpu_custom_call" | custom-call | tf_op jit(solution)/shard_map/pallas_call | solution.py:491
  23.7 15.0 %pmax.14 = f32[8,128]{1,0:T(8,128)S(1)} all-reduce(f32[8,128]{1,0:T(8,128)S(1)} %get-tuple-element.36), channel_id=1, replica_groups=mesh['pts_0'=8,'pts_1'=2,'dir'=16,'freq'=2] {'pts_0'}, use_global_device_ids=true, to_apply=%region_0.0 | all-reduce | flops 1024 | bytes 8192 | tf_op jit(solution)/shard_map/pmax | solution.py:566
  38.6 2.5 %pmax.15.note_ref = f32[8,128]{1,0:T(8,128)S(1)} all-reduce(f32[8,128]{1,0:T(8,128)S(1)} %pmax.14), channel_id=1, replica_groups=mesh['pts_0'=8,'pts_1'=2,'dir'=16,'freq'=2] {'pts_1'}, use_global_device_ids=true, to_apply=%region_1.0 | all-reduce | flops 1024 | bytes 8192 | tf_op jit(solution)/shard_map/pmax | solution.py:566
  41.1 3.4 %collective-permute-start.2 = (f32[136,128]{1,0:T(8,128)S(1)}, f32[136,128]{1,0:T(8,128)S(1)}, u32[]{:S(2)}, u32[]{:S(2)}) collective-permute-start(f32[136,128]{1,0:T(8,128)S(1)} %pad_maximum_fusion), channel_id=1, source_target_pairs={{0,1},{1,0},{2,3},{3,2},{4,5},{5,4},{6,7},{7,6},{8,9},{9,8},{10,11... | collective-permute-start | bytes 208904 | tf_op jit(solution)/shard_map/ppermute | solution.py:567
  44.5 0.7 slice.3
  45.9 0.0 copy-done.7
  45.9 0.0 copy-done.9
  45.9 0.0 copy-done.8
  45.9 11.6 %collective-permute-done.2.other_ref = f32[136,128]{1,0:T(8,128)S(1)} collective-permute-done((f32[136,128]{1,0:T(8,128)S(1)}, f32[136,128]{1,0:T(8,128)S(1)}, u32[]{:S(2)}, u32[]{:S(2)}) %collective-permute-start.2) | collective-permute-done | bytes 69664 | tf_op jit(solution)/shard_map/ppermute | solution.py:567
  57.5 0.0 collective-permute-done.3.left_ref
  57.5 0.0 collective-permute-done.4.right_ref
  57.5 0.0 copy-done.1
  57.5 0.0 copy-start.4
  57.5 0.0 copy-start.6
  57.5 3.1 %shard_map.93 = (f32[1024,128]{1,0:T(8,128)S(1)}, f32[512,128]{1,0:T(8,128)S(1)}) custom-call(s32[4]{0:T(128)S(1)} %pad_add_fusion.meta, s32[8]{0:T(128)S(1)} %copy-done.2, f32[8,128]{1,0:T(8,128)S(1)} %pmax.15.note_ref, f32[136,128]{1,0:T(8,128)S(1)} %collective-permute-done.2.other_ref, f32[3072,128]{1,0:T(8,128)} %bitcast.38, f32[32,128]{1,0:T(8,128)S(1)} %bitcast.50, ...), custom_call_target="tpu_custom_call" | custom-call | tf_op jit(solution)/shard_map/pallas_call | solution.py:491
  60.6 0.0 copy-start
  60.6 2.1 %collective-permute-start.5 = (f32[512,128]{1,0:T(8,128)S(1)}, f32[512,128]{1,0:T(8,128)S(1)}, u32[]{:S(2)}, u32[]{:S(2)}) collective-permute-start(f32[512,128]{1,0:T(8,128)S(1)} %get-tuple-element.46), channel_id=1, source_target_pairs={{0,1},{1,0},{2,3},{3,2},{4,5},{5,4},{6,7},{7,6},{8,9},{9,8},{10,11... | collective-permute-start | bytes 786440 | tf_op jit(solution)/shard_map/ppermute | solution.py:598
  62.7 0.0 copy-done.4
  62.7 0.0 copy-done.6
  62.7 4.0 %shard_map.94.far_ref = f32[2048,128]{1,0:T(8,128)S(1)} custom-call(s32[4]{0:T(128)S(1)} %pad_add_fusion.meta, s32[8]{0:T(128)S(1)} %copy-done.2, f32[8,128]{1,0:T(8,128)S(1)} %pmax.15.note_ref, f32[136,128]{1,0:T(8,128)S(1)} %collective-permute-done.2.other_ref, f32[3072,128]{1,0:T(8,128)} %bitcast.39, f32[32,128]{1,0:T(8,128)S(1)} %bitcast.51, ...), custom_call_target="tpu_custom_call" | custom-call | tf_op jit(solution)/shard_map/pallas_call | solution.py:491
  66.8 0.0 copy-done
  66.8 2.8 %shard_map.95.rest_1_ = f32[3072,128]{1,0:T(8,128)} custom-call(s32[4]{0:T(128)S(1)} %pad_add_fusion.meta, s32[8]{0:T(128)S(1)} %copy-done.2, f32[8,128]{1,0:T(8,128)S(1)} %pmax.15.note_ref, f32[136,128]{1,0:T(8,128)S(1)} %collective-permute-done.2.other_ref, f32[1024,128]{1,0:T(8,128)S(1)} %get-tuple-element.44.near_ref, ...), custom_call_target="tpu_custom_call" | custom-call | tf_op jit(solution)/shard_map/pallas_call | solution.py:491
  69.5 1.2 %collective-permute-done.5.rest_0_ = f32[512,128]{1,0:T(8,128)S(1)} collective-permute-done((f32[512,128]{1,0:T(8,128)S(1)}, f32[512,128]{1,0:T(8,128)S(1)}, u32[]{:S(2)}, u32[]{:S(2)}) %collective-permute-start.5) | collective-permute-done | bytes 262176 | tf_op jit(solution)/shard_map/ppermute | solution.py:598
  70.7 2.4 %shard_map.96 = f32[3072,128]{1,0:T(8,128)} custom-call(s32[4]{0:T(128)S(1)} %pad_add_fusion.meta, s32[8]{0:T(128)S(1)} %copy-done.2, f32[8,128]{1,0:T(8,128)S(1)} %pmax.15.note_ref, f32[136,128]{1,0:T(8,128)S(1)} %collective-permute-done.2.other_ref, f32[1024,128]{1,0:T(8,128)S(1)} %get-tuple-element.44.near_ref, ...), custom_call_target="tpu_custom_call", output_to_operand_aliasing={{}: (10, {})} | custom-call | tf_op jit(solution)/shard_map/pallas_call | solution.py:491
  (3 shorter events, 0.0 us)
Async XLA Ops:
  0.0 21.4 %copy-start.10 = (f32[256]{0:T(256)S(1)}, f32[256]{0:T(256)}, u32[]{:S(2)}) copy-start(f32[256]{0:T(256)} %constant.25.clone.table) | copy-start | bytes 3076
  0.0 45.9 %copy-start.7 = (s32[4096]{0:T(1024)S(1)}, s32[4096]{0:T(1024)}, u32[]{:S(2)}) copy-start(s32[4096]{0:T(1024)} %param.17) | copy-start | bytes 49156
  0.0 45.9 %copy-start.9 = (f32[4096]{0:T(1024)S(1)}, f32[4096]{0:T(1024)}, u32[]{:S(2)}) copy-start(f32[4096]{0:T(1024)} %param.16) | copy-start | bytes 49156
  0.0 45.9 %copy-start.8 = (f32[4096]{0:T(1024)S(1)}, f32[4096]{0:T(1024)}, u32[]{:S(2)}) copy-start(f32[4096]{0:T(1024)} %param.12) | copy-start | bytes 49156
  0.0 21.3 %copy-start.2 = (s32[8]{0:T(128)S(1)}, s32[8]{0:T(128)}, u32[]{:S(2)}) copy-start(s32[8]{0:T(128)} %count.9) | copy-start | bytes 100
  6.1 51.4 %copy-start.1 = (f32[24,4096]{1,0:T(8,128)S(1)}, f32[24,4096]{1,0:T(8,128)}, u32[]{:S(2)}) copy-start(f32[24,4096]{1,0:T(8,128)} %param.13) | copy-start | bytes 1179652
  6.2 51.3 %collective-permute-start.3 = (f32[96,2048]{1,0:T(8,128)}, f32[96,2048]{1,0:T(8,128)S(1)}, u32[]{:S(2)}, u32[]{:S(2)}) collective-permute-start(f32[96,2048]{1,0:T(8,128)} %get-tuple-element.40), channel_id=1, source_target_pairs={{0,2},{2,4},{4,6},{6,8},{8,10},{10,12},{12,14},{14,16},{16,18},{18... | collective-permute-start | bytes 2359304 | tf_op jit(solution)/shard_map/ppermute | solution.py:535
  12.4 45.1 %collective-permute-start.4 = (f32[96,2048]{1,0:T(8,128)S(1)}, f32[96,2048]{1,0:T(8,128)S(1)}, u32[]{:S(2)}, u32[]{:S(2)}) collective-permute-start(f32[96,2048]{1,0:T(8,128)S(1)} %get-tuple-element.41), channel_id=1, source_target_pairs={{2,0},{4,2},{6,4},{8,6},{10,8},{12,10},{14,12},{16,14},{18,16},{20... | collective-permute-start | bytes 2359304 | tf_op jit(solution)/shard_map/ppermute | solution.py:535
  41.1 16.4 %collective-permute-start.2 = (f32[136,128]{1,0:T(8,128)S(1)}, f32[136,128]{1,0:T(8,128)S(1)}, u32[]{:S(2)}, u32[]{:S(2)}) collective-permute-start(f32[136,128]{1,0:T(8,128)S(1)} %pad_maximum_fusion), channel_id=1, source_target_pairs={{0,1},{1,0},{2,3},{3,2},{4,5},{5,4},{6,7},{7,6},{8,9},{9,8},{10,11... | collective-permute-start | bytes 208904 | tf_op jit(solution)/shard_map/ppermute | solution.py:567
  57.5 5.2 %copy-start.4 = (f32[96,2048]{1,0:T(8,128)S(1)}, f32[96,2048]{1,0:T(8,128)}, u32[]{:S(2)}) copy-start(f32[96,2048]{1,0:T(8,128)} %get-tuple-element.42.left_hbm) | copy-start | bytes 2359300
  57.5 5.2 %copy-start.6 = (f32[96,2048]{1,0:T(8,128)S(1)}, f32[96,2048]{1,0:T(8,128)}, u32[]{:S(2)}) copy-start(f32[96,2048]{1,0:T(8,128)} %get-tuple-element.43.right_hbm) | copy-start | bytes 2359300
  60.6 6.1 %copy-start = (f32[24,4096]{1,0:T(8,128)S(1)}, f32[24,4096]{1,0:T(8,128)}, u32[]{:S(2)}) copy-start(f32[24,4096]{1,0:T(8,128)} %param.14) | copy-start | bytes 1179652
  60.6 10.1 %collective-permute-start.5 = (f32[512,128]{1,0:T(8,128)S(1)}, f32[512,128]{1,0:T(8,128)S(1)}, u32[]{:S(2)}, u32[]{:S(2)}) collective-permute-start(f32[512,128]{1,0:T(8,128)S(1)} %get-tuple-element.46), channel_id=1, source_target_pairs={{0,1},{1,0},{2,3},{3,2},{4,5},{5,4},{6,7},{7,6},{8,9},{9,8},{10,11... | collective-permute-start | bytes 786440 | tf_op jit(solution)/shard_map/ppermute | solution.py:598

commit v3 on v2

--- a/solution.py
+++ b/solution.py
@@ -14,14 +14,15 @@
 DIR = 64
 KMAX = 4
 BLK = 512
-SLOTS = 256
+GROUPS = 13
 EPSILON = 1e-06
 LANES = 128
 F_LOC = 24
 D_LOC = 4
 TILES = 32
+SIDE = D_LOC * 24
 ROWS = TILES * D_LOC
-VMEM_LIMIT = 24 * 1024 * 1024
+VMEM_LIMIT = 12 * 1024 * 1024
 LOW = -3.0e38
 
 f32, bf16, i32 = jnp.float32, jnp.bfloat16, jnp.int32
@@ -76,28 +77,37 @@
     return at
 
 
-def ranks(mask):
-    on = jnp.where(mask, 1.0, 0.0).astype(f32).astype(bf16)
+def ranks(first_mask, second_mask):
+    first = jnp.where(first_mask, 1.0, 0.0).astype(f32)
+    second = jnp.where(second_mask, 1.0, 0.0).astype(f32)
+    on = jnp.concatenate([first, second], axis=0).astype(bf16)
+    none = jnp.zeros((TILES, LANES), f32)
+    spread = jnp.concatenate([first, none, second, none], axis=0).astype(bf16)
     row, col = iota((LANES, LANES), 0), iota((LANES, LANES), 1)
     before = jnp.where(row < col, 1.0, 0.0).astype(bf16)
+    earlier = jnp.where((row < col) & (row // 64 == col // 64), 1.0, 0.0).astype(bf16)
     ones = jnp.ones((LANES, LANES), bf16)
-    r, c = iota((TILES, TILES), 0), iota((TILES, TILES), 1)
-    earlier = jnp.where((c < r) & (r // 4 == c // 4), 1.0, 0.0).astype(bf16)
+    r, c = iota((2 * TILES, 2 * TILES), 0), iota((2 * TILES, 2 * TILES), 1)
+    above = jnp.where((c < r) & (r // TILES == c // TILES), 1.0, 0.0).astype(bf16)
     inner = jnp.dot(on, before, preferred_element_type=f32)
     number = jnp.dot(on, ones, preferred_element_type=f32)
-    offset = jnp.dot(earlier, on, preferred_element_type=f32)
+    offset = jnp.dot(above, on, preferred_element_type=f32)
     offset = jnp.dot(offset.astype(bf16), ones, preferred_element_type=f32)
-    return inner.astype(i32), offset.astype(i32), number.astype(i32)
+    along = lax.dot_general(ones[:16], spread, (((1,), (1,)), ((), ())), preferred_element_type=f32)
+    along = jnp.dot(along.astype(bf16), earlier, preferred_element_type=f32)[0:8]
+    return inner.astype(i32), offset.astype(i32), number.astype(i32), along.astype(i32)
 
 
 def gather(x, index):
     return jnp.take_along_axis(x, index, axis=1)
 
 
-def packing(mask, wave, source_ref, slot_ref):
-    inner, offset, number = ranks(mask)
-    lane = iota((TILES, LANES), 1)
-    code = jnp.where(mask, (lane - inner) * 128 + lane + 65536, 0)
+def packing(up_mask, down_mask, source_ref, code_ref, group_ref):
+    inner, offset, number, along = ranks(up_mask, down_mask)
+    lane = iota((2 * TILES, LANES), 1)
+    mark = lane * 129 + 65536
+    on = jnp.concatenate([jnp.where(m, 1, 0) for m in (up_mask, down_mask)], axis=0)
+    code = jnp.where(on == 1, mark - inner * 128, 0)
     for bit in range(7):
         step = 1 << bit
         far = pltpu.roll(code, LANES - step, 1)
@@ -106,39 +116,82 @@
         code = jnp.where(comes, far - (128 << bit), jnp.where(goes, 0, code))
     source = gather((code & 127).astype(f32), (lane - offset) & 127)
     source_ref[...] = source.astype(i32)
-    slot = lane + ((offset - lane + 127) >> 7) * LANES
-    slot_ref[...] = jnp.where(slot < offset + number, slot - wave * SLOTS, -1)
-
-
-def pack_block(x_ref, block, source, slot, outs):
-    for d in range(D_LOC):
-        for g in range(3):
-            x = [x_ref[pl.ds(g * 8 * ROWS + (4 * block + j) * D_LOC + d, 8, stride=ROWS), :] for j in range(4)]
-            for s_ref, k_ref, out in zip(source, slot, outs):
-                low = jnp.zeros((8, LANES), f32)
-                high = jnp.zeros((8, LANES), f32)
-                for j in range(4):
-                    tile = pl.ds(4 * block + j, 1)
-                    taken = gather(x[j], jnp.broadcast_to(s_ref[tile, :], (8, LANES)))
-                    half = jnp.broadcast_to(k_ref[tile, :], (8, LANES)) >> 7
-                    low = jnp.where(half == 0, taken, low)
-                    high = jnp.where(half == 1, taken, high)
-                rows = slice((d * 3 + g) * 8, (d * 3 + g) * 8 + 8)
-                out[rows, pl.ds(pl.multiple_of(block * SLOTS, SLOTS), LANES)] = low
-                out[rows, pl.ds(pl.multiple_of(block * SLOTS + LANES, LANES), LANES)] = high
-
-
-def more_kernel(meta, table, x_ref, bath_ref, slope_ref, wet_ref, up_ref, down_ref, *scratch):
+    start = offset & 127
+    here = (lane >= start) & (lane < start + number)
+    crosses = (start + number) >= LANES
+    code_ref[...] = jnp.where(here, 1, 0) + jnp.where(crosses, 2, 0)
+    group_ref[...] = along >> 7
+
+
+def pack_kernel(wave, meta, table, bath_hbm, slope_hbm, wet_hbm, x_hbm, up_hbm, down_hbm, *rest):
+    if wave == 0:
+        edge_ref, *rest = rest
+    *rest, x_ref = rest
+    bath_ref, slope_ref, wet_ref, up_ref, down_ref, sems, in_sems, up_sems, down_sems, at_sems, edge_sem, *rest = rest
+    source_ref, code_ref, group_ref, group_at = rest
+    begin, size = ((0, GROUPS), (GROUPS, TILES - GROUPS))[wave]
+
+    def arrival(g):
+        rows = pl.ds(g * 8 * ROWS, 8 * ROWS)
+        return pltpu.make_async_copy(x_hbm.at[rows, :], x_ref.at[rows, :], in_sems.at[g])
+
+    def departures(g):
+        rows, columns = pl.ds(g * 8 * D_LOC, 8 * D_LOC), pl.ds(begin * LANES, size * LANES)
+        return (
+            pltpu.make_async_copy(up_ref.at[rows, columns], up_hbm.at[rows, :], up_sems.at[g]),
+            pltpu.make_async_copy(down_ref.at[rows, columns], down_hbm.at[rows, :], down_sems.at[g]),
+        )
+
+    copies = fetch(((bath_hbm, bath_ref), (slope_hbm, slope_ref), (wet_hbm, wet_ref)), sems)
+    for g in range(3):
+        arrival(g).start()
+    if wave == 0:
+        (kept,) = fetch(((rows_of(x_hbm, True, meta), edge_ref),), edge_sem)
+    for ref in (up_ref, down_ref):
+        ref[:, begin * LANES : (begin + size) * LANES] = jnp.zeros((SIDE, size * LANES), f32)
+    for copy in copies:
+        copy.wait()
     slope = slope_ref[...]
     at = masks(table, bath_ref[...], wet_ref[...].astype(f32), jnp.sin(slope), jnp.cos(slope))
-    packing(at(D_LOC * meta[0] + D_LOC)[0], 1, scratch[0], scratch[1])
-    packing(at(D_LOC * meta[0])[1], 1, scratch[2], scratch[3])
-
-    def one(block, carry):
-        pack_block(x_ref, block, scratch[::2], scratch[1::2], (up_ref, down_ref))
-        return carry
-
-    lax.fori_loop(0, 8, one, 0)
+    packing(at(D_LOC * meta[0] + D_LOC)[0], at(D_LOC * meta[0])[1], source_ref, code_ref, group_ref)
+    (copy,) = fetch(((group_ref, group_at),), at_sems)
+    copy.wait()
+    sides = (up_ref, down_ref)
+    for g in range(3):
+        arrival(g).wait()
+
+        def one(tile, partial):
+            x = [x_ref[pl.ds(g * 8 * ROWS + tile * D_LOC + d, 8, stride=ROWS), :] for d in range(D_LOC)]
+            out = []
+            for k, ref in enumerate(sides):
+                index = jnp.broadcast_to(source_ref[pl.ds(k * TILES + tile, 1), :], (8, LANES))
+                flags = jnp.broadcast_to(code_ref[pl.ds(k * TILES + tile, 1), :], (8, LANES))
+                here, crosses = (flags & 1) != 0, flags >= 2
+                columns = pl.ds(pl.multiple_of(group_at[0, k * 64 + tile] * LANES, LANES), LANES)
+                for d in range(D_LOC):
+                    taken = gather(x[d], index)
+                    full = jnp.where(here, taken, partial[k * D_LOC + d])
+                    ref[(g * D_LOC + d) * 8 : (g * D_LOC + d + 1) * 8, columns] = full
+                    out.append(jnp.where(crosses, taken, full))
+            return tuple(out)
+
+        def four(i, partial):
+            for j in range(4):
+                partial = one(4 * i + j, partial)
+            return partial
+
+        partial = lax.fori_loop(0, TILES // 4, four, (jnp.zeros((8, LANES), f32),) * (2 * D_LOC))
+        for k, ref in enumerate(sides):
+            columns = pl.ds(pl.multiple_of(group_at[0, k * 64 + TILES] * LANES, LANES), LANES)
+            for d in range(D_LOC):
+                ref[(g * D_LOC + d) * 8 : (g * D_LOC + d + 1) * 8, columns] = partial[k * D_LOC + d]
+        for copy in departures(g):
+            copy.start()
+    for g in range(3):
+        for copy in departures(g):
+            copy.wait()
+    if wave == 0:
+        kept.wait()
 
 
 def part(edge, meta):
@@ -157,44 +210,7 @@
     return copies
 
 
-def pack_kernel(meta, table, bath_hbm, slope_hbm, wet_hbm, x_hbm, up_hbm, down_hbm, bath_ref, slope_ref, wet_ref, x_ref, up_ref, down_ref, sems, in_sems, up_sems, down_sems, *scratch):
-    def arrival(c):
-        rows = pl.ds(pl.multiple_of(c * 8 * D_LOC, 8 * D_LOC), 8 * D_LOC)
-        return pltpu.make_async_copy(x_hbm.at[:, rows, :], x_ref.at[:, rows, :], in_sems.at[c])
-
-    def departures(c):
-        columns = pl.ds(pl.multiple_of(c * 2 * SLOTS, 2 * SLOTS), 2 * SLOTS)
-        return (
-            pltpu.make_async_copy(up_ref.at[:, columns], up_hbm.at[:, columns], up_sems.at[c]),
-            pltpu.make_async_copy(down_ref.at[:, columns], down_hbm.at[:, columns], down_sems.at[c]),
-        )
-
-    copies = fetch(((bath_hbm, bath_ref), (slope_hbm, slope_ref), (wet_hbm, wet_ref)), sems)
-    for c in range(4):
-        arrival(c).start()
-    for copy in copies:
-        copy.wait()
-    slope = slope_ref[...]
-    at = masks(table, bath_ref[...], wet_ref[...].astype(f32), jnp.sin(slope), jnp.cos(slope))
-    packing(at(D_LOC * meta[0] + D_LOC)[0], 0, scratch[0], scratch[1])
-    packing(at(D_LOC * meta[0])[1], 0, scratch[2], scratch[3])
-    flat = x_ref.reshape(F_LOC * ROWS, LANES)
-
-    def two(c, carry):
-        arrival(c).wait()
-        for block in (2 * c, 2 * c + 1):
-            pack_block(flat, block, scratch[::2], scratch[1::2], (up_ref, down_ref))
-        for copy in departures(c):
-            copy.start()
-        return carry
-
-    lax.fori_loop(0, 4, two, 0)
-    for c in range(4):
-        for copy in departures(c):
-            copy.wait()
-
-
-def note_kernel(meta, table, count, bath_hbm, slope_hbm, wet_hbm, heading_hbm, refr_hbm, shift_hbm, note_ref, halo_ref, sine_ref, wave_ref, shift_rim_ref, bath_ref, slope_ref, wet_ref, heading_ref, refr_ref, shift_ref, sems, turn_row, shift_row, refr_row, marks):
+def note_kernel(meta, table, count, bath_hbm, slope_hbm, wet_hbm, heading_hbm, refr_hbm, shift_hbm, note_ref, halo_ref, group_ref, sine_ref, wave_ref, shift_rim_ref, bath_ref, slope_ref, wet_ref, heading_ref, refr_ref, shift_ref, sems, turn_row, shift_row, refr_row, marks):
     copies = fetch(
         (
             (bath_hbm, bath_ref),
@@ -244,14 +260,14 @@
         marks[2 * i * TILES : (2 * i + 1) * TILES, :] = jnp.where(low, 1.0, 0.0).astype(f32)
         marks[(2 * i + 1) * TILES : (2 * i + 2) * TILES, :] = jnp.where(high, 1.0, 0.0).astype(f32)
     ones = jnp.ones((LANES, LANES), bf16)
-    group = jnp.where(iota((LANES, 4 * LANES), 0) == iota((LANES, 4 * LANES), 1) // 4, 1.0, 0.0).astype(bf16)
-    per_block = jnp.dot(group, marks[...].astype(bf16), preferred_element_type=f32)
-    per_block = jnp.dot(per_block.astype(bf16), ones, preferred_element_type=f32)
+    group = jnp.where(iota((16, 16 * TILES), 0) == iota((16, 16 * TILES), 1) // TILES, 1.0, 0.0).astype(bf16)
+    per_side = jnp.dot(group, marks[...].astype(bf16), preferred_element_type=f32)
+    per_side = jnp.dot(per_side.astype(bf16), ones, preferred_element_type=f32)
 
     weight = wet * sin_peak
     row, lane = iota((8, LANES), 0), iota((8, LANES), 1)
     note = jnp.where(row == 0, jnp.where(lane == 0, jnp.max(turn), jnp.max(shift)), LOW)
-    note = jnp.where((row == 0) & (lane == 2), jnp.max(per_block), note)
+    note = jnp.where((row == 0) & (lane == 2), jnp.max(per_side), note)
     refr_row[0:1, :] = ends[0] * weight[0:1, :]
     refr_row[1:2, :] = ends[1] * weight[TILES - 1 : TILES, :]
     mine = lane == meta[2]
@@ -272,8 +288,10 @@
         row = jnp.where(meta[1] == 0, 7 - m, m)
         shift_rim_ref[m * TILES : (m + 1) * TILES, :] = shift_ref[pl.ds(first * 256 + row, TILES, stride=8), :]
 
-    unpacking(at(D_LOC * meta[0])[0], halo_ref, 0)
-    unpacking(at(D_LOC * meta[0] + D_LOC)[1], halo_ref, 2)
+    inner, offset, _, along = ranks(at(D_LOC * meta[0])[0], at(D_LOC * meta[0] + D_LOC)[1])
+    halo_ref[: 2 * TILES, :] = (inner + offset) & 127
+    halo_ref[2 * TILES :, :] = jnp.where(iota((2 * TILES, LANES), 1) >= (offset & 127), 1, 0)
+    group_ref[...] = along >> 7
     for k in range(FACES):
         sine_ref[k * TILES : (k + 1) * TILES, :] = face_sine(table, D_LOC * meta[0] - KMAX + 1 + k, sin_s, cos_s)
     sign = jnp.where(meta[1] == 0, 0.5, -0.5)
@@ -313,48 +331,44 @@
     return counts.astype(f32)
 
 
-def unpacking(mask, ref, at):
-    inner, offset, _ = ranks(mask)
-    ref[at * TILES : (at + 1) * TILES, :] = (inner + offset) & 127
-    ref[(at + 1) * TILES : (at + 2) * TILES, :] = (offset - iota((TILES, LANES), 1) + 127) >> 7
-
-
-def turn_kernel(edge, meta, count, note_ref, other_ref, x_hbm, bath_ref, wet_ref, refr_ref, halo_ref, sines, left_ref, right_ref, left_hbm, right_hbm, *rest):
+def turn_kernel(edge, meta, count, group_at, note_ref, other_ref, x_hbm, bath_ref, wet_ref, refr_ref, halo_ref, sines, left_ref, right_ref, left_hbm, right_hbm, *rest):
     if edge:
         y_ref, rim_ref, *rest = rest
     else:
         y_ref, *rest = rest
-    speed, left_more, right_more, x_ref, sems = rest
-    (copy,) = fetch(((rows_of(x_hbm, edge, meta), x_ref),), sems)
+    if edge:
+        x_ref = x_hbm
+    else:
+        *rest, x_ref, sems = rest
+        (copy,) = fetch(((rows_of(x_hbm, edge, meta), x_ref),), sems)
+    speed, left_wide, right_wide = rest
     note = jnp.maximum(note_ref[...], other_ref[0:8, :])
     scale = 0.5 / (jnp.full((TILES, LANES), largest_turn(note), f32) + EPSILON)
     wet = wet_ref[...].astype(f32)
     speed[...] = full_gradient(meta, note, bath_ref[...]) * wet * scale * COS_HALF / block_counts(count)
     first, groups = part(edge, meta)
-    copy.wait()
-    overflow = jnp.max(jnp.where(iota((1, LANES), 1) == 2, note[0:1, :], LOW)) > SLOTS
-
-    def halo(wide, d, g, block, refs, tile):
-        ref, more, at = refs
+    if not edge:
+        copy.wait()
+    overflow = jnp.max(jnp.where(iota((1, LANES), 1) == 2, note[0:1, :], LOW)) > GROUPS * LANES
+
+    def halo(wide, d, g, refs, tile):
+        ref, side = refs
+        most = TILES - 1 if wide else GROUPS - 1
 
         def eight(k):
             return jnp.broadcast_to(halo_ref[pl.ds(k * TILES + tile, 1), :], (8, LANES))
 
-        def slots(source, half, row):
-            lanes = pl.ds(pl.multiple_of(block * SLOTS + half * LANES, LANES), LANES)
-            return source[pl.ds(pl.multiple_of(row, 8), 8), lanes]
-
-        half = eight(at + 1)
-        row = (d * 3 + first + g) * 8
-        values = jnp.where(half == 0, slots(ref, 0, row), slots(ref, 1, row))
-        if wide:
-            values = jnp.where(half == 2, slots(more, 0, row), values)
-            values = jnp.where(half == 3, slots(more, 1, row), values)
-        return gather(values, eight(at))
+        def slots(group):
+            lanes = pl.ds(pl.multiple_of(jnp.minimum(group, most) * LANES, LANES), LANES)
+            return ref[pl.ds(pl.multiple_of(((first + g) * D_LOC + d) * 8, 8), 8), lanes]
+
+        group = group_at[0, side * 64 + tile]
+        values = jnp.where(eight(2 + side) == 1, slots(group), slots(group + 1))
+        return gather(values, eight(side))
 
     def sweep(wide, block, carry):
-        low = (left_ref, left_more, 0)
-        high = (right_ref, right_more, 2)
+        low = (left_wide if wide else left_ref, 0)
+        high = (right_wide if wide else right_ref, 1)
         steps = count[block]
         for kmax in range(1, KMAX + 1):
 
@@ -373,11 +387,11 @@
                         for c in range(KMAX - kmax, D_LOC + KMAX + kmax):
                             d = c % D_LOC
                             if c < KMAX:
-                                cells.append(halo(wide, d, g, block, low, tile))
+                                cells.append(halo(wide, d, g, low, tile))
                             elif c < KMAX + D_LOC:
                                 cells.append(x_ref[pl.ds(g * 8 * ROWS + tile * D_LOC + d, 8, stride=ROWS), :])
                             else:
-                                cells.append(halo(wide, d, g, block, high, tile))
+                                cells.append(halo(wide, d, g, high, tile))
                         face = [base * v for v in sine]
                         plus = [jnp.maximum(v, 0.0) for v in face]
                         minus = [jnp.minimum(v, 0.0) for v in face]
@@ -394,8 +408,9 @@
 
     @pl.when(overflow)
     def _():
-        pltpu.sync_copy(left_hbm, left_more)
-        pltpu.sync_copy(right_hbm, right_more)
+        for ref, more, whole in ((left_ref, left_hbm, left_wide), (right_ref, right_hbm, right_wide)):
+            whole[:, : GROUPS * LANES] = ref[...]
+            pltpu.sync_copy(more, whole.at[:, GROUPS * LANES :])
         lax.fori_loop(0, 8, functools.partial(sweep, True), 0)
 
     @pl.when(jnp.logical_not(overflow))
@@ -527,7 +542,7 @@
     ring_down = [((i + 1) % count, i) for i in range(count)]
     swap = [(0, 1), (1, 0)]
 
-    wave = [shape(D_LOC * F_LOC, 8 * SLOTS)] * 2
+    waves_of = [[shape(SIDE, GROUPS * LANES)] * 2, [shape(SIDE, (TILES - GROUPS) * LANES)] * 2]
     row = pltpu.VMEM((TILES, LANES), f32)
     row_int = pltpu.VMEM((TILES, LANES), i32)
 
@@ -537,21 +552,32 @@
     small = [row, row, row_int]
     coefs = pltpu.VMEM((3 * TILES * 8, LANES), f32)
     dma = pltpu.SemaphoreType.DMA
-    packed = pltpu.VMEM((D_LOC * F_LOC, 8 * SLOTS), f32)
-    up, down = call(
-        pack_kernel,
-        wave,
-        [SMEM, SMEM] + [HBM] * 4,
-        small + [pltpu.VMEM((F_LOC, ROWS, LANES), f32), packed, packed, dma((3,)), dma((4,)), dma((4,)), dma((4,))] + [row_int] * 4,
-        (meta, table, *in_hbm(bath, slope, wet, x.reshape(F_LOC, ROWS, LANES))),
-        out_specs=[ANY, ANY],
-    )
+    packed = pltpu.VMEM((SIDE, (TILES + 1) * LANES), f32)
+    wide = pltpu.VMEM((SIDE, TILES * LANES), f32)
+
+    def pack(wave):
+        vmem_x = pltpu.VMEM((F_LOC * ROWS, LANES), f32)
+        both = pltpu.VMEM((2 * TILES, LANES), i32)
+        return call(
+            functools.partial(pack_kernel, wave),
+            waves_of[wave] + ([pltpu.VMEM((8 * ROWS, LANES), f32)] if wave == 0 else []),
+            [SMEM, SMEM] + [HBM] * 4,
+            small
+            + [packed, packed, dma((3,)), dma((3,)), dma((3,)), dma((3,)), dma((1,)), dma((1,))]
+            + [both, both, pltpu.VMEM((8, LANES), i32), pltpu.SMEM((8, LANES), i32)]
+            + [vmem_x],
+            (meta, table, *in_hbm(bath, slope, wet, x)),
+            out_specs=[ANY, ANY] + ([VMEM] if wave == 0 else []),
+        )
+
+    up, down, x_edge = pack(0)
     left, right = exchange(up, down)
-    note, halo, sines, waves, shift_rim = call(
+    note, halo, groups_at, sines, waves, shift_rim = call(
         note_kernel,
         [
             shape(8, LANES),
             jax.ShapeDtypeStruct((4 * TILES, LANES), i32),
+            jax.ShapeDtypeStruct((8, LANES), i32),
             shape(FACES * TILES, LANES),
             shape(ROWS, LANES),
             shape(KMAX * TILES, LANES),
@@ -567,31 +593,22 @@
     other = lax.ppermute(jnp.concatenate([note, shift_rim], axis=0), "freq", swap)
 
     def second_wave():
-        return exchange(
-            *call(
-                more_kernel,
-                wave,
-                [SMEM, SMEM] + [VMEM] * 4,
-                [row_int] * 4,
-                (meta, table, x, bath, slope, wet),
-            )
-        )
+        return exchange(*pack(1))
 
     def no_wave():
-        return tuple(call(lambda *refs: None, wave, [], [], (), out_specs=[ANY, ANY]))
-
-    left_more, right_more = lax.cond(note[0, 2] > SLOTS, second_wave, no_wave)
+        return tuple(call(lambda *refs: None, waves_of[1], [], [], (), out_specs=[ANY, ANY]))
+
+    left_more, right_more = lax.cond(note[0, 2] > GROUPS * LANES, second_wave, no_wave)
 
     def turn(edge):
         groups = 1 if edge else 2
         outs = [shape(groups * 8 * ROWS, LANES)] + ([shape(KMAX * ROWS, LANES)] if edge else [])
-        own = [pltpu.VMEM((groups * 8 * ROWS, LANES), f32), dma((1,))]
         return call(
             functools.partial(turn_kernel, edge),
             outs,
-            [SMEM] * 2 + [VMEM] * 2 + [HBM] + [VMEM] * 7 + [ANY] * 2,
-            [row, packed, packed] + own,
-            (meta, substeps, note, other, *in_hbm(x), bath, wet, refr, halo, sines, left, right, left_more, right_more),
+            [SMEM] * 3 + [VMEM] * 2 + [VMEM if edge else HBM] + [VMEM] * 7 + [HBM] * 2,
+            [row, wide, wide] + ([] if edge else [pltpu.VMEM((groups * 8 * ROWS, LANES), f32), dma((1,))]),
+            (meta, substeps, groups_at, note, other, *([x_edge] if edge else in_hbm(x)), bath, wet, refr, halo, sines, left, right, *in_hbm(left_more, right_more)),
         )
 
     near, rim = turn(True)

time: 73.6 us -> 68 us (0.924)
  waiting for transfers between devices: 12.8 us -> 5.98 us
  Pallas kernels: 20.6 us -> 21.8 us
    ppermute x1, waiting for transfers between devices: 11.6 us -> 5.37 us  [local(): lax.ppermute(jnp.concatenate([note, shift_rim], axis=0), 'freq', swap)]
    pallas_call x7, Pallas kernels: 20.6 us -> 21.8 us  [call(): pl.pallas_call(body, out_shape=outs, in_specs=in_specs, out_specs=out_spe...]
  transfers between devices with their start and end apart: 4 -> 4, of which waited for: 2 -> 2; matrix products, arithmetic and copies ran while one was open for 1% -> 1% of each run, Pallas kernels for 12% -> 14%
where the time goes in v3:
time: 68 us; the launch traced here: 67.3 us
  Pallas kernels  21.8 us (32%)
  starting transfers between devices  20.6 us (30%)
  blocking collectives  17.4 us (26%)
  waiting for transfers between devices  5.98 us (9%)
  between operations  0.82 us (1%)
    pallas_call x7, Pallas kernels, call(): pl.pallas_call(body, out_shape=outs, in_specs=in_specs, out_specs=out_spe...  21.8 us
    pmax x2, blocking collectives, local(): note = lax.pmax(note, axis)  17.4 us
    ppermute x1, starting transfers between devices, exchange(): lax.ppermute(down, 'dir', ring_down)  8.96 us
    ppermute x1, starting transfers between devices, exchange(): lax.ppermute(up, 'dir', ring_up)  6.22 us
    ppermute x1, waiting for transfers between devices, local(): lax.ppermute(jnp.concatenate([note, shift_rim], axis=0), 'freq', swap)  5.37 us
    ppermute x1, starting transfers between devices, local(): lax.ppermute(jnp.concatenate([note, shift_rim], axis=0), 'freq', swap)  3.37 us
    ppermute x1, starting transfers between devices, local(): other_rim = lax.ppermute(rim, 'freq', swap)  2.05 us
  transfers between devices with their start and end apart: 4, of which 2 were waited for; matrix products, arithmetic and copies ran while one was open for 1% of the time, Pallas kernels for 14%

profile of v3, /device:TPU:56, one launch (start us, length us, event | category | flops | bytes accessed | tf_op | source)
XLA Modules:
  0.0 67.3 jit_solution(14270999458474056166)
XLA Ops:
  0.0 0.0 copy-start.7
  0.0 0.0 copy-start.5
  0.0 0.0 copy-start.6
  0.0 0.0 copy-start.2
  0.0 0.1 pad_add_fusion.meta
  0.1 7.2 %shard_map.92 = (f32[96,1664]{1,0:T(8,128)}, f32[96,1664]{1,0:T(8,128)S(1)}, f32[1024,128]{1,0:T(8,128)S(1)}) custom-call(s32[4]{0:T(128)S(1)} %pad_add_fusion.meta, f32[256]{0:T(256)} %constant.25.clone.table, f32[32,128]{1,0:T(8,128)} %bitcast.44, f32[32,128]{1,0:T(8,128)} %bitcast.49, s32[32,128]{1,0:T(8,128)} %bitcast.37, f32[3072,128]{1,0:T(8,128)} %bitcast.34), custom_call_target="tpu_custom_call" | custom-call | tf_op jit(solution)/shard_map/pallas_call | solution.py:506
  7.3 0.0 copy-start
  7.3 6.2 %collective-permute-start.3 = (f32[96,1664]{1,0:T(8,128)}, f32[96,1664]{1,0:T(8,128)S(1)}, u32[]{:S(2)}, u32[]{:S(2)}) collective-permute-start(f32[96,1664]{1,0:T(8,128)} %get-tuple-element.44), channel_id=1, source_target_pairs={{0,2},{2,4},{4,6},{6,8},{8,10},{10,12},{12,14},{14,16},{16,18},{18... | collective-permute-start | bytes 1916936 | tf_op jit(solution)/shard_map/ppermute | solution.py:550
  13.6 9.0 %collective-permute-start.4 = (f32[96,1664]{1,0:T(8,128)S(1)}, f32[96,1664]{1,0:T(8,128)S(1)}, u32[]{:S(2)}, u32[]{:S(2)}) collective-permute-start(f32[96,1664]{1,0:T(8,128)S(1)} %get-tuple-element.45), channel_id=1, source_target_pairs={{2,0},{4,2},{6,4},{8,6},{10,8},{12,10},{14,12},{16,14},{18,16},{20... | collective-permute-start | bytes 1916936 | tf_op jit(solution)/shard_map/ppermute | solution.py:550
  22.5 0.0 copy-done.7
  22.6 0.0 copy-done.2
  22.6 2.3 %shard_map.91 = (f32[8,128]{1,0:T(8,128)S(1)}, s32[128,128]{1,0:T(8,128)S(1)}, s32[8,128]{1,0:T(8,128)S(1)}, f32[352,128]{1,0:T(8,128)S(1)}, f32[128,128]{1,0:T(8,128)S(1)}, /*index=5*/f32[128,128]{1,0:T(8,128)S(1)}) custom-call(s32[4]{0:T(128)S(1)} %pad_add_fusion.meta, f32[256]{0:T(256)S(1)} %copy-done.7, s32[8]{0:T(128)S(1)} %copy-done.2, ...), custom_call_target="tpu_custom_call" | custom-call | tf_op jit(solution)/shard_map/pallas_call | solution.py:506
  24.8 15.0 %pmax.14 = f32[8,128]{1,0:T(8,128)S(1)} all-reduce(f32[8,128]{1,0:T(8,128)S(1)} %get-tuple-element.38), channel_id=1, replica_groups=mesh['pts_0'=8,'pts_1'=2,'dir'=16,'freq'=2] {'pts_0'}, use_global_device_ids=true, to_apply=%region_0.0 | all-reduce | flops 1024 | bytes 8192 | tf_op jit(solution)/shard_map/pmax | solution.py:592
  39.8 2.5 %pmax.15.note_ref = f32[8,128]{1,0:T(8,128)S(1)} all-reduce(f32[8,128]{1,0:T(8,128)S(1)} %pmax.14), channel_id=1, replica_groups=mesh['pts_0'=8,'pts_1'=2,'dir'=16,'freq'=2] {'pts_1'}, use_global_device_ids=true, to_apply=%region_1.0 | all-reduce | flops 1024 | bytes 8192 | tf_op jit(solution)/shard_map/pmax | solution.py:592
  42.3 3.4 %collective-permute-start.2 = (f32[136,128]{1,0:T(8,128)S(1)}, f32[136,128]{1,0:T(8,128)S(1)}, u32[]{:S(2)}, u32[]{:S(2)}) collective-permute-start(f32[136,128]{1,0:T(8,128)S(1)} %pad_maximum_fusion), channel_id=1, source_target_pairs={{0,1},{1,0},{2,3},{3,2},{4,5},{5,4},{6,7},{7,6},{8,9},{9,8},{10,11... | collective-permute-start | bytes 208904 | tf_op jit(solution)/shard_map/ppermute | solution.py:593
  45.7 0.6 slice.3
  46.9 0.0 copy-done.5
  46.9 0.0 copy-done.6
  46.9 5.4 %collective-permute-done.2.other_ref = f32[136,128]{1,0:T(8,128)S(1)} collective-permute-done((f32[136,128]{1,0:T(8,128)S(1)}, f32[136,128]{1,0:T(8,128)S(1)}, u32[]{:S(2)}, u32[]{:S(2)}) %collective-permute-start.2) | collective-permute-done | bytes 69664 | tf_op jit(solution)/shard_map/ppermute | solution.py:593
  52.3 0.0 collective-permute-done.3.left_ref
  52.3 0.0 collective-permute-done.4.right_ref
  52.3 0.0 copy-done
  52.3 2.4 %shard_map.93 = (f32[1024,128]{1,0:T(8,128)S(1)}, f32[512,128]{1,0:T(8,128)S(1)}) custom-call(s32[4]{0:T(128)S(1)} %pad_add_fusion.meta, s32[8]{0:T(128)S(1)} %copy-done.2, s32[8,128]{1,0:T(8,128)S(1)} %get-tuple-element.40.group_at, f32[8,128]{1,0:T(8,128)S(1)} %pmax.15.note_ref, f32[136,128]{1,0:T(8,128)S(1)} %collective-permute-done.2.other_ref, ...), custom_call_target="tpu_custom_call" | custom-call | tf_op jit(solution)/shard_map/pallas_call | solution.py:506
  54.8 0.0 copy-start.1
  54.8 2.1 %collective-permute-start.5 = (f32[512,128]{1,0:T(8,128)S(1)}, f32[512,128]{1,0:T(8,128)S(1)}, u32[]{:S(2)}, u32[]{:S(2)}) collective-permute-start(f32[512,128]{1,0:T(8,128)S(1)} %get-tuple-element.50), channel_id=1, source_target_pairs={{0,1},{1,0},{2,3},{3,2},{4,5},{5,4},{6,7},{7,6},{8,9},{9,8},{10,11... | collective-permute-start | bytes 786440 | tf_op jit(solution)/shard_map/ppermute | solution.py:615
  56.8 4.6 %shard_map.94.far_ref = f32[2048,128]{1,0:T(8,128)S(1)} custom-call(s32[4]{0:T(128)S(1)} %pad_add_fusion.meta, s32[8]{0:T(128)S(1)} %copy-done.2, s32[8,128]{1,0:T(8,128)S(1)} %get-tuple-element.40.group_at, f32[8,128]{1,0:T(8,128)S(1)} %pmax.15.note_ref, f32[136,128]{1,0:T(8,128)S(1)} %collective-permute-done.2.other_ref, f32[3072,128]{1,0:T(8,128)} %bitcast.36, ...), custom_call_target="tpu_custom_call" | custom-call | tf_op jit(solution)/shard_map/pallas_call | solution.py:506
  61.5 0.0 copy-done.1
  61.5 2.8 %shard_map.95.rest_1_ = f32[3072,128]{1,0:T(8,128)} custom-call(s32[4]{0:T(128)S(1)} %pad_add_fusion.meta, s32[8]{0:T(128)S(1)} %copy-done.2, f32[8,128]{1,0:T(8,128)S(1)} %pmax.15.note_ref, f32[136,128]{1,0:T(8,128)S(1)} %collective-permute-done.2.other_ref, f32[1024,128]{1,0:T(8,128)S(1)} %get-tuple-element.48.near_ref, ...), custom_call_target="tpu_custom_call" | custom-call | tf_op jit(solution)/shard_map/pallas_call | solution.py:506
  64.3 0.6 collective-permute-done.5.rest_0_
  64.9 2.4 %shard_map.96 = f32[3072,128]{1,0:T(8,128)} custom-call(s32[4]{0:T(128)S(1)} %pad_add_fusion.meta, s32[8]{0:T(128)S(1)} %copy-done.2, f32[8,128]{1,0:T(8,128)S(1)} %pmax.15.note_ref, f32[136,128]{1,0:T(8,128)S(1)} %collective-permute-done.2.other_ref, f32[1024,128]{1,0:T(8,128)S(1)} %get-tuple-element.48.near_ref, ...), custom_call_target="tpu_custom_call", output_to_operand_aliasing={{}: (10, {})} | custom-call | tf_op jit(solution)/shard_map/pallas_call | solution.py:506
  (3 shorter events, 0.0 us)
Async XLA Ops:
  0.0 22.5 %copy-start.7 = (f32[256]{0:T(256)S(1)}, f32[256]{0:T(256)}, u32[]{:S(2)}) copy-start(f32[256]{0:T(256)} %constant.25.clone.table) | copy-start | bytes 3076
  0.0 46.9 %copy-start.5 = (s32[4096]{0:T(1024)S(1)}, s32[4096]{0:T(1024)}, u32[]{:S(2)}) copy-start(s32[4096]{0:T(1024)} %param.17) | copy-start | bytes 49156
  0.0 46.9 %copy-start.6 = (f32[4096]{0:T(1024)S(1)}, f32[4096]{0:T(1024)}, u32[]{:S(2)}) copy-start(f32[4096]{0:T(1024)} %param.12) | copy-start | bytes 49156
  0.0 22.5 %copy-start.2 = (s32[8]{0:T(128)S(1)}, s32[8]{0:T(128)}, u32[]{:S(2)}) copy-start(s32[8]{0:T(128)} %count.9) | copy-start | bytes 100
  7.3 45.0 %copy-start = (f32[24,4096]{1,0:T(8,128)S(1)}, f32[24,4096]{1,0:T(8,128)}, u32[]{:S(2)}) copy-start(f32[24,4096]{1,0:T(8,128)} %param.13) | copy-start | bytes 1179652
  7.3 45.0 %collective-permute-start.3 = (f32[96,1664]{1,0:T(8,128)}, f32[96,1664]{1,0:T(8,128)S(1)}, u32[]{:S(2)}, u32[]{:S(2)}) collective-permute-start(f32[96,1664]{1,0:T(8,128)} %get-tuple-element.44), channel_id=1, source_target_pairs={{0,2},{2,4},{4,6},{6,8},{8,10},{10,12},{12,14},{14,16},{16,18},{18... | collective-permute-start | bytes 1916936 | tf_op jit(solution)/shard_map/ppermute | solution.py:550
  13.6 38.7 %collective-permute-start.4 = (f32[96,1664]{1,0:T(8,128)S(1)}, f32[96,1664]{1,0:T(8,128)S(1)}, u32[]{:S(2)}, u32[]{:S(2)}) collective-permute-start(f32[96,1664]{1,0:T(8,128)S(1)} %get-tuple-element.45), channel_id=1, source_target_pairs={{2,0},{4,2},{6,4},{8,6},{10,8},{12,10},{14,12},{16,14},{18,16},{20... | collective-permute-start | bytes 1916936 | tf_op jit(solution)/shard_map/ppermute | solution.py:550
  42.3 10.0 %collective-permute-start.2 = (f32[136,128]{1,0:T(8,128)S(1)}, f32[136,128]{1,0:T(8,128)S(1)}, u32[]{:S(2)}, u32[]{:S(2)}) collective-permute-start(f32[136,128]{1,0:T(8,128)S(1)} %pad_maximum_fusion), channel_id=1, source_target_pairs={{0,1},{1,0},{2,3},{3,2},{4,5},{5,4},{6,7},{7,6},{8,9},{9,8},{10,11... | collective-permute-start | bytes 208904 | tf_op jit(solution)/shard_map/ppermute | solution.py:593
  54.8 6.7 %copy-start.1 = (f32[24,4096]{1,0:T(8,128)S(1)}, f32[24,4096]{1,0:T(8,128)}, u32[]{:S(2)}) copy-start(f32[24,4096]{1,0:T(8,128)} %param.14) | copy-start | bytes 1179652
  54.8 10.1 %collective-permute-start.5 = (f32[512,128]{1,0:T(8,128)S(1)}, f32[512,128]{1,0:T(8,128)S(1)}, u32[]{:S(2)}, u32[]{:S(2)}) collective-permute-start(f32[512,128]{1,0:T(8,128)S(1)} %get-tuple-element.50), channel_id=1, source_target_pairs={{0,1},{1,0},{2,3},{3,2},{4,5},{5,4},{6,7},{7,6},{8,9},{9,8},{10,11... | collective-permute-start | bytes 786440 | tf_op jit(solution)/shard_map/ppermute | solution.py:615

commit v4 on v3

--- a/solution.py
+++ b/solution.py
@@ -102,8 +102,10 @@
     return jnp.take_along_axis(x, index, axis=1)
 
 
-def packing(up_mask, down_mask, source_ref, code_ref, group_ref):
+def packing(up_mask, down_mask, source_ref, code_ref, group_ref, send_groups):
     inner, offset, number, along = ranks(up_mask, down_mask)
+    group_ref[...] = along >> 7
+    send_groups()
     lane = iota((2 * TILES, LANES), 1)
     mark = lane * 129 + 65536
     on = jnp.concatenate([jnp.where(m, 1, 0) for m in (up_mask, down_mask)], axis=0)
@@ -120,7 +122,6 @@
     here = (lane >= start) & (lane < start + number)
     crosses = (start + number) >= LANES
     code_ref[...] = jnp.where(here, 1, 0) + jnp.where(crosses, 2, 0)
-    group_ref[...] = along >> 7
 
 
 def pack_kernel(wave, meta, table, bath_hbm, slope_hbm, wet_hbm, x_hbm, up_hbm, down_hbm, *rest):
@@ -153,31 +154,33 @@
         copy.wait()
     slope = slope_ref[...]
     at = masks(table, bath_ref[...], wet_ref[...].astype(f32), jnp.sin(slope), jnp.cos(slope))
-    packing(at(D_LOC * meta[0] + D_LOC)[0], at(D_LOC * meta[0])[1], source_ref, code_ref, group_ref)
-    (copy,) = fetch(((group_ref, group_at),), at_sems)
+    copy = pltpu.make_async_copy(group_ref, group_at, at_sems.at[0])
+    packing(at(D_LOC * meta[0] + D_LOC)[0], at(D_LOC * meta[0])[1], source_ref, code_ref, group_ref, copy.start)
     copy.wait()
     sides = (up_ref, down_ref)
     for g in range(3):
         arrival(g).wait()
 
-        def one(tile, partial):
-            x = [x_ref[pl.ds(g * 8 * ROWS + tile * D_LOC + d, 8, stride=ROWS), :] for d in range(D_LOC)]
-            out = []
-            for k, ref in enumerate(sides):
-                index = jnp.broadcast_to(source_ref[pl.ds(k * TILES + tile, 1), :], (8, LANES))
-                flags = jnp.broadcast_to(code_ref[pl.ds(k * TILES + tile, 1), :], (8, LANES))
-                here, crosses = (flags & 1) != 0, flags >= 2
-                columns = pl.ds(pl.multiple_of(group_at[0, k * 64 + tile] * LANES, LANES), LANES)
-                for d in range(D_LOC):
-                    taken = gather(x[d], index)
-                    full = jnp.where(here, taken, partial[k * D_LOC + d])
-                    ref[(g * D_LOC + d) * 8 : (g * D_LOC + d + 1) * 8, columns] = full
-                    out.append(jnp.where(crosses, taken, full))
-            return tuple(out)
-
         def four(i, partial):
-            for j in range(4):
-                partial = one(4 * i + j, partial)
+            tiles = [4 * i + j for j in range(4)]
+            taken, flags = [], []
+            for tile in tiles:
+                x = [x_ref[pl.ds(g * 8 * ROWS + tile * D_LOC + d, 8, stride=ROWS), :] for d in range(D_LOC)]
+                for k in range(2):
+                    index = jnp.broadcast_to(source_ref[pl.ds(k * TILES + tile, 1), :], (8, LANES))
+                    flags.append(jnp.broadcast_to(code_ref[pl.ds(k * TILES + tile, 1), :], (8, LANES)))
+                    taken.append([gather(x[d], index) for d in range(D_LOC)])
+            for j, tile in enumerate(tiles):
+                out = []
+                for k, ref in enumerate(sides):
+                    here, crosses = (flags[2 * j + k] & 1) != 0, flags[2 * j + k] >= 2
+                    columns = pl.ds(pl.multiple_of(group_at[0, k * 64 + tile] * LANES, LANES), LANES)
+                    for d in range(D_LOC):
+                        value = taken[2 * j + k][d]
+                        full = jnp.where(here, value, partial[k * D_LOC + d])
+                        ref[(g * D_LOC + d) * 8 : (g * D_LOC + d + 1) * 8, columns] = full
+                        out.append(jnp.where(crosses, value, full))
+                partial = tuple(out)
             return partial
 
         partial = lax.fori_loop(0, TILES // 4, four, (jnp.zeros((8, LANES), f32),) * (2 * D_LOC))
@@ -374,6 +377,7 @@
 
             @pl.when(steps == kmax)
             def _():
+                done = []
                 for j in range(4):
                     tile = 4 * block + j
                     drive = speed[pl.ds(tile, 1), :]
@@ -401,8 +405,13 @@
                                 plus[step + i] * cells[i] + minus[step + i] * cells[i + 1] for i in range(n)
                             ]
                             cells = [cells[i + 1] - (flux[i + 1] - flux[i]) for i in range(n - 1)]
+                        done.append((g, tile, cells))
+                    if j % (4 // groups) != 4 // groups - 1:
+                        continue
+                    for g, at_tile, cells in done:
                         for d in range(D_LOC):
-                            y_ref[pl.ds(g * 8 * ROWS + tile * D_LOC + d, 8, stride=ROWS), :] = cells[d]
+                            y_ref[pl.ds(g * 8 * ROWS + at_tile * D_LOC + d, 8, stride=ROWS), :] = cells[d]
+                    done = []
 
         return carry
 
@@ -480,20 +489,32 @@
                 count_out = 8 if rim else 16
                 for i in range(count_out):
                     row = i if lower else count_out - 1 - i
-                    out_ref[pl.ds(row * ROWS + offset, 8), :] = cells[i] * mask_wet
-
+                    out_ref[row, pl.ds(offset, 8), :] = cells[i] * mask_wet
+
+        return carry
+
+    first, groups = part(rim, meta)
+
+    def departure(c):
+        rows = pl.ds(pl.multiple_of(c * 32, 32), 32)
+        freqs = pl.ds(first * 8, groups * 8)
+        return pltpu.make_async_copy(out_ref.at[:, rows, :], out_hbm.at[freqs, rows, :], sems.at[c])
+
+    def quarter(lower, c, carry):
+        lax.fori_loop(4 * c, 4 * c + 4, functools.partial(one, lower), 0)
+        departure(c).start()
         return carry
 
     @pl.when(meta[1] == 0)
     def _():
-        lax.fori_loop(0, TILES // 2, functools.partial(one, True), 0)
+        lax.fori_loop(0, 4, functools.partial(quarter, True), 0)
 
     @pl.when(meta[1] == 1)
     def _():
-        lax.fori_loop(0, TILES // 2, functools.partial(one, False), 0)
-
-    (copy,) = fetch(((out_ref, rows_of(out_hbm, rim, meta)),), sems)
-    copy.wait()
+        lax.fori_loop(0, 4, functools.partial(quarter, False), 0)
+
+    for c in range(4):
+        departure(c).wait()
 
 
 SMEM = pl.BlockSpec(memory_space=pltpu.SMEM)
@@ -619,9 +640,9 @@
         groups = 1 if rim else 2
         (out,) = call(
             functools.partial(shift_kernel, rim),
-            [shape(F_LOC * ROWS, LANES)],
+            [shape(F_LOC, ROWS, LANES)],
             [SMEM] * 2 + [VMEM] * 7 + [VMEM, ANY][: len(more)],
-            [row, pltpu.VMEM((groups * 8 * ROWS, LANES), f32), dma((1,))],
+            [row, pltpu.VMEM((groups * 8, ROWS, LANES), f32), dma((4,))],
             (meta, substeps, note, other, near, far, shift, waves, wet, *more),
             out_specs=[ANY],
             aliases={10: 0} if rim else None,

time: 68 us -> 68 us (level)
  Pallas kernels: 21.8 us -> 21.1 us
where the time goes in v4:
time: 68 us; the launch traced here: 67.1 us
  Pallas kernels  21.1 us (31%)
  starting transfers between devices  20.6 us (30%)
  blocking collectives  17.4 us (26%)
  waiting for transfers between devices  6.42 us (9%)
  between operations  0.82 us (1%)
    pallas_call x7, Pallas kernels, call(): pl.pallas_call(body, out_shape=outs, in_specs=in_specs, out_specs=out_spe...  21.1 us
    pmax x2, blocking collectives, local(): note = lax.pmax(note, axis)  17.4 us
    ppermute x1, starting transfers between devices, exchange(): lax.ppermute(down, 'dir', ring_down)  8.96 us
    ppermute x1, starting transfers between devices, exchange(): lax.ppermute(up, 'dir', ring_up)  6.22 us
    ppermute x1, waiting for transfers between devices, local(): lax.ppermute(jnp.concatenate([note, shift_rim], axis=0), 'freq', swap)  5.37 us
    ppermute x1, starting transfers between devices, local(): lax.ppermute(jnp.concatenate([note, shift_rim], axis=0), 'freq', swap)  3.37 us
    ppermute x1, starting transfers between devices, local(): other_rim = lax.ppermute(rim, 'freq', swap)  2.05 us
  transfers between devices with their start and end apart: 4, of which 2 were waited for; matrix products, arithmetic and copies ran while one was open for 1% of the time, Pallas kernels for 14%

profile of v4, /device:TPU:56, one launch (start us, length us, event | category | flops | bytes accessed | tf_op | source)
XLA Modules:
  0.0 67.1 jit_solution(10582556177388135389)
XLA Ops:
  0.0 0.0 copy-start.7
  0.0 0.0 copy-start.5
  0.0 0.0 copy-start.6
  0.0 0.0 copy-start.2
  0.0 0.1 pad_add_fusion.meta
  0.1 7.2 %shard_map.92 = (f32[96,1664]{1,0:T(8,128)}, f32[96,1664]{1,0:T(8,128)S(1)}, f32[1024,128]{1,0:T(8,128)S(1)}) custom-call(s32[4]{0:T(128)S(1)} %pad_add_fusion.meta, f32[256]{0:T(256)} %constant.25.clone.table, f32[32,128]{1,0:T(8,128)} %bitcast.44, f32[32,128]{1,0:T(8,128)} %bitcast.49, s32[32,128]{1,0:T(8,128)} %bitcast.37, f32[3072,128]{1,0:T(8,128)} %bitcast.34), custom_call_target="tpu_custom_call" | custom-call | tf_op jit(solution)/shard_map/pallas_call | solution.py:527
  7.3 0.0 copy-start
  7.3 6.2 %collective-permute-start.3 = (f32[96,1664]{1,0:T(8,128)}, f32[96,1664]{1,0:T(8,128)S(1)}, u32[]{:S(2)}, u32[]{:S(2)}) collective-permute-start(f32[96,1664]{1,0:T(8,128)} %get-tuple-element.44), channel_id=1, source_target_pairs={{0,2},{2,4},{4,6},{6,8},{8,10},{10,12},{12,14},{14,16},{16,18},{18... | collective-permute-start | bytes 1916936 | tf_op jit(solution)/shard_map/ppermute | solution.py:571
  13.6 9.0 %collective-permute-start.4 = (f32[96,1664]{1,0:T(8,128)S(1)}, f32[96,1664]{1,0:T(8,128)S(1)}, u32[]{:S(2)}, u32[]{:S(2)}) collective-permute-start(f32[96,1664]{1,0:T(8,128)S(1)} %get-tuple-element.45), channel_id=1, source_target_pairs={{2,0},{4,2},{6,4},{8,6},{10,8},{12,10},{14,12},{16,14},{18,16},{20... | collective-permute-start | bytes 1916936 | tf_op jit(solution)/shard_map/ppermute | solution.py:571
  22.5 0.0 copy-done.7
  22.6 0.0 copy-done.2
  22.6 2.3 %shard_map.91 = (f32[8,128]{1,0:T(8,128)S(1)}, s32[128,128]{1,0:T(8,128)S(1)}, s32[8,128]{1,0:T(8,128)S(1)}, f32[352,128]{1,0:T(8,128)S(1)}, f32[128,128]{1,0:T(8,128)S(1)}, /*index=5*/f32[128,128]{1,0:T(8,128)S(1)}) custom-call(s32[4]{0:T(128)S(1)} %pad_add_fusion.meta, f32[256]{0:T(256)S(1)} %copy-done.7, s32[8]{0:T(128)S(1)} %copy-done.2, ...), custom_call_target="tpu_custom_call" | custom-call | tf_op jit(solution)/shard_map/pallas_call | solution.py:527
  24.8 15.0 %pmax.14 = f32[8,128]{1,0:T(8,128)S(1)} all-reduce(f32[8,128]{1,0:T(8,128)S(1)} %get-tuple-element.38), channel_id=1, replica_groups=mesh['pts_0'=8,'pts_1'=2,'dir'=16,'freq'=2] {'pts_0'}, use_global_device_ids=true, to_apply=%region_0.0 | all-reduce | flops 1024 | bytes 8192 | tf_op jit(solution)/shard_map/pmax | solution.py:613
  39.8 2.5 %pmax.15.note_ref = f32[8,128]{1,0:T(8,128)S(1)} all-reduce(f32[8,128]{1,0:T(8,128)S(1)} %pmax.14), channel_id=1, replica_groups=mesh['pts_0'=8,'pts_1'=2,'dir'=16,'freq'=2] {'pts_1'}, use_global_device_ids=true, to_apply=%region_1.0 | all-reduce | flops 1024 | bytes 8192 | tf_op jit(solution)/shard_map/pmax | solution.py:613
  42.3 3.4 %collective-permute-start.2 = (f32[136,128]{1,0:T(8,128)S(1)}, f32[136,128]{1,0:T(8,128)S(1)}, u32[]{:S(2)}, u32[]{:S(2)}) collective-permute-start(f32[136,128]{1,0:T(8,128)S(1)} %pad_maximum_fusion), channel_id=1, source_target_pairs={{0,1},{1,0},{2,3},{3,2},{4,5},{5,4},{6,7},{7,6},{8,9},{9,8},{10,11... | collective-permute-start | bytes 208904 | tf_op jit(solution)/shard_map/ppermute | solution.py:614
  45.7 0.6 slice.3
  46.9 0.0 copy-done.5
  46.9 0.0 copy-done.6
  46.9 5.4 %collective-permute-done.2.other_ref = f32[136,128]{1,0:T(8,128)S(1)} collective-permute-done((f32[136,128]{1,0:T(8,128)S(1)}, f32[136,128]{1,0:T(8,128)S(1)}, u32[]{:S(2)}, u32[]{:S(2)}) %collective-permute-start.2) | collective-permute-done | bytes 69664 | tf_op jit(solution)/shard_map/ppermute | solution.py:614
  52.3 0.0 collective-permute-done.3.left_ref
  52.3 0.0 collective-permute-done.4.right_ref
  52.3 0.0 copy-done
  52.3 2.4 %shard_map.93 = (f32[1024,128]{1,0:T(8,128)S(1)}, f32[512,128]{1,0:T(8,128)S(1)}) custom-call(s32[4]{0:T(128)S(1)} %pad_add_fusion.meta, s32[8]{0:T(128)S(1)} %copy-done.2, s32[8,128]{1,0:T(8,128)S(1)} %get-tuple-element.40.group_at, f32[8,128]{1,0:T(8,128)S(1)} %pmax.15.note_ref, f32[136,128]{1,0:T(8,128)S(1)} %collective-permute-done.2.other_ref, ...), custom_call_target="tpu_custom_call" | custom-call | tf_op jit(solution)/shard_map/pallas_call | solution.py:527
  54.7 0.0 copy-start.1
  54.7 2.1 %collective-permute-start.5 = (f32[512,128]{1,0:T(8,128)S(1)}, f32[512,128]{1,0:T(8,128)S(1)}, u32[]{:S(2)}, u32[]{:S(2)}) collective-permute-start(f32[512,128]{1,0:T(8,128)S(1)} %get-tuple-element.50), channel_id=1, source_target_pairs={{0,1},{1,0},{2,3},{3,2},{4,5},{5,4},{6,7},{7,6},{8,9},{9,8},{10,11... | collective-permute-start | bytes 786440 | tf_op jit(solution)/shard_map/ppermute | solution.py:636
  56.8 4.4 %shard_map.94.far_ref = f32[2048,128]{1,0:T(8,128)S(1)} custom-call(s32[4]{0:T(128)S(1)} %pad_add_fusion.meta, s32[8]{0:T(128)S(1)} %copy-done.2, s32[8,128]{1,0:T(8,128)S(1)} %get-tuple-element.40.group_at, f32[8,128]{1,0:T(8,128)S(1)} %pmax.15.note_ref, f32[136,128]{1,0:T(8,128)S(1)} %collective-permute-done.2.other_ref, f32[3072,128]{1,0:T(8,128)} %bitcast.36, ...), custom_call_target="tpu_custom_call" | custom-call | tf_op jit(solution)/shard_map/pallas_call | solution.py:527
  61.2 0.0 copy-done.1
  61.2 2.5 %shard_map.95.rest_1_ = f32[24,128,128]{2,1,0:T(8,128)} custom-call(s32[4]{0:T(128)S(1)} %pad_add_fusion.meta, s32[8]{0:T(128)S(1)} %copy-done.2, f32[8,128]{1,0:T(8,128)S(1)} %pmax.15.note_ref, f32[136,128]{1,0:T(8,128)S(1)} %collective-permute-done.2.other_ref, f32[1024,128]{1,0:T(8,128)S(1)} %get-tuple-element.48.near_ref, ...), custom_call_target="tpu_custom_call" | custom-call | tf_op jit(solution)/shard_map/pallas_call | solution.py:527
  63.7 1.0 %collective-permute-done.5.rest_0_ = f32[512,128]{1,0:T(8,128)S(1)} collective-permute-done((f32[512,128]{1,0:T(8,128)S(1)}, f32[512,128]{1,0:T(8,128)S(1)}, u32[]{:S(2)}, u32[]{:S(2)}) %collective-permute-start.5) | collective-permute-done | bytes 262176 | tf_op jit(solution)/shard_map/ppermute | solution.py:636
  64.8 2.3 %shard_map.96 = f32[24,128,128]{2,1,0:T(8,128)} custom-call(s32[4]{0:T(128)S(1)} %pad_add_fusion.meta, s32[8]{0:T(128)S(1)} %copy-done.2, f32[8,128]{1,0:T(8,128)S(1)} %pmax.15.note_ref, f32[136,128]{1,0:T(8,128)S(1)} %collective-permute-done.2.other_ref, f32[1024,128]{1,0:T(8,128)S(1)} %get-tuple-element.48.near_ref, ...), custom_call_target="tpu_custom_call", output_to_operand_aliasing={{}: (10, {})} | custom-call | tf_op jit(solution)/shard_map/pallas_call | solution.py:527
  (3 shorter events, 0.0 us)
Async XLA Ops:
  0.0 22.5 %copy-start.7 = (f32[256]{0:T(256)S(1)}, f32[256]{0:T(256)}, u32[]{:S(2)}) copy-start(f32[256]{0:T(256)} %constant.25.clone.table) | copy-start | bytes 3076
  0.0 46.9 %copy-start.5 = (s32[4096]{0:T(1024)S(1)}, s32[4096]{0:T(1024)}, u32[]{:S(2)}) copy-start(s32[4096]{0:T(1024)} %param.17) | copy-start | bytes 49156
  0.0 46.9 %copy-start.6 = (f32[4096]{0:T(1024)S(1)}, f32[4096]{0:T(1024)}, u32[]{:S(2)}) copy-start(f32[4096]{0:T(1024)} %param.12) | copy-start | bytes 49156
  0.0 22.5 %copy-start.2 = (s32[8]{0:T(128)S(1)}, s32[8]{0:T(128)}, u32[]{:S(2)}) copy-start(s32[8]{0:T(128)} %count.9) | copy-start | bytes 100
  7.3 45.0 %copy-start = (f32[24,4096]{1,0:T(8,128)S(1)}, f32[24,4096]{1,0:T(8,128)}, u32[]{:S(2)}) copy-start(f32[24,4096]{1,0:T(8,128)} %param.13) | copy-start | bytes 1179652
  7.3 45.0 %collective-permute-start.3 = (f32[96,1664]{1,0:T(8,128)}, f32[96,1664]{1,0:T(8,128)S(1)}, u32[]{:S(2)}, u32[]{:S(2)}) collective-permute-start(f32[96,1664]{1,0:T(8,128)} %get-tuple-element.44), channel_id=1, source_target_pairs={{0,2},{2,4},{4,6},{6,8},{8,10},{10,12},{12,14},{14,16},{16,18},{18... | collective-permute-start | bytes 1916936 | tf_op jit(solution)/shard_map/ppermute | solution.py:571
  13.6 38.7 %collective-permute-start.4 = (f32[96,1664]{1,0:T(8,128)S(1)}, f32[96,1664]{1,0:T(8,128)S(1)}, u32[]{:S(2)}, u32[]{:S(2)}) collective-permute-start(f32[96,1664]{1,0:T(8,128)S(1)} %get-tuple-element.45), channel_id=1, source_target_pairs={{2,0},{4,2},{6,4},{8,6},{10,8},{12,10},{14,12},{16,14},{18,16},{20... | collective-permute-start | bytes 1916936 | tf_op jit(solution)/shard_map/ppermute | solution.py:571
  42.3 10.0 %collective-permute-start.2 = (f32[136,128]{1,0:T(8,128)S(1)}, f32[136,128]{1,0:T(8,128)S(1)}, u32[]{:S(2)}, u32[]{:S(2)}) collective-permute-start(f32[136,128]{1,0:T(8,128)S(1)} %pad_maximum_fusion), channel_id=1, source_target_pairs={{0,1},{1,0},{2,3},{3,2},{4,5},{5,4},{6,7},{7,6},{8,9},{9,8},{10,11... | collective-permute-start | bytes 208904 | tf_op jit(solution)/shard_map/ppermute | solution.py:614
  54.7 6.5 %copy-start.1 = (f32[24,4096]{1,0:T(8,128)S(1)}, f32[24,4096]{1,0:T(8,128)}, u32[]{:S(2)}) copy-start(f32[24,4096]{1,0:T(8,128)} %param.14) | copy-start | bytes 1179652
  54.7 10.1 %collective-permute-start.5 = (f32[512,128]{1,0:T(8,128)S(1)}, f32[512,128]{1,0:T(8,128)S(1)}, u32[]{:S(2)}, u32[]{:S(2)}) collective-permute-start(f32[512,128]{1,0:T(8,128)S(1)} %get-tuple-element.50), channel_id=1, source_target_pairs={{0,1},{1,0},{2,3},{3,2},{4,5},{5,4},{6,7},{7,6},{8,9},{9,8},{10,11... | collective-permute-start | bytes 786440 | tf_op jit(solution)/shard_map/ppermute | solution.py:636
